TPU v7x, 256 devices: a whole 4x4x8 slice. The times are simulated.
256 devices in a mesh: rep: 16 (over z_lo, x), exp: 16 (over y, z_hi, core).
Axes of the slice: x: 4, y: 4, z: 8 (z_hi: 2, z_lo: 4; z = z_hi * 4 + z_lo), core: 2. Of those that a mesh axis runs over, the one named last changes fastest.
Arguments:
- w_in: bfloat16 [16, 768, 1536], P('exp'), may hold values from -0.21875 to 0.21875
- w_out: bfloat16 [16, 1536, 768], P('exp'), may hold values from -0.15625 to 0.15625
- mom_in: float32 [16, 768, 1536], P('exp', 'rep'), may hold values from -0.024 to 0.024
- mom_out: float32 [16, 1536, 768], P('exp', 'rep'), may hold values from -0.024 to 0.024
- frames: bfloat16 [16, 2, 2048, 768], P('rep', None, 'exp'), may hold values from -6 to 6
- targets: bfloat16 [16, 2, 2048, 768], P('rep', None, 'exp'), may hold values from -6 to 6
- routes: int32 [16, 2, 2048, 2], P('rep', None, 'exp'), may hold values from 0 to 15, all different within a row; in each aligned block of 128 rows (0 to 127, 128 to 255, ..., all dimensions but the last counted through in order) at most 32 rows name the same one
- gates: float32 [16, 2, 2048, 2], P('rep', None, 'exp'), may hold values from 0.1 to 0.9
Outputs:
- new_w_in: bfloat16 [16, 768, 1536], P('exp')
- new_w_out: bfloat16 [16, 1536, 768], P('exp')
- new_mom_in: float32 [16, 768, 1536], P('exp', 'rep')
- new_mom_out: float32 [16, 1536, 768], P('exp', 'rep')
Inputs may be any that keep to these rules, and one draw needn't show every extreme that they name: `routes`: within the 128 rows of one device and one inner step no expert is named by more than 32 rows, a bound that some block reaches; the two experts of a frame differ.
All inputs are finite; a program needn't handle non-finite values.
Results may differ from a plain program's by a relative error of at most 0.0075.
Values may be sent and summed in bfloat16 or wider, within the bound.
No kernel may reach another device: no remote copies, remote signals or barrier semaphores. Data moves between devices by JAX's collectives and lax.ppermute only.
A program may use at most 128 MiB of HBM per device.

v0:
```python
import jax
import jax.numpy as jnp
from jax import lax
from jax.sharding import PartitionSpec as P

STEPS = 2


def slot_table(route_rows, experts):
    flat = route_rows.reshape(-1)
    onehot = (flat[:, None] == jnp.arange(experts, dtype=jnp.int32)[None, :]).astype(jnp.int32)
    running = jnp.cumsum(onehot, axis=0)
    return (jnp.sum(running * onehot, axis=1) - 1).reshape(route_rows.shape)


def adamw(theta, first, second, grad, count):
    first = 0.9 * first + 0.1 * grad
    second = 0.95 * second + 0.05 * grad * grad
    ratio = first / (1.0 - 0.9**count) / (jnp.sqrt(second / (1.0 - 0.95**count)) + 0.01)
    return (theta - 0.004 * (ratio + 0.1 * theta), first, second)


def contract_rows(left, right):
    return lax.dot_general(
        left, right, (((0,), (0,)), ((), ())), preferred_element_type=jnp.float32
    )


def outer_update(start_w, momentum, summed, replicas):
    averaged = summed / replicas
    new_momentum = 0.9 * momentum + averaged
    rows = momentum.shape[1]
    first_row = lax.axis_index("rep") * rows
    own_rows = lax.dynamic_slice_in_dim(start_w, first_row, rows, 1).astype(jnp.float32)
    return ((own_rows - 0.7 * (averaged + 0.9 * new_momentum)).astype(jnp.bfloat16), new_momentum)


def per_device(w_in, w_out, mom_in, mom_out, frames, targets, routes, gates):
    experts = lax.axis_size("exp") * w_in.shape[0]
    width = w_in.shape[1]
    tok_rows = frames.shape[2]
    capacity = 4 * tok_rows // experts
    theta_in = w_in.astype(jnp.float32)
    theta_out = w_out.astype(jnp.float32)
    first_in = jnp.zeros_like(theta_in)
    second_in = jnp.zeros_like(theta_in)
    first_out = jnp.zeros_like(theta_out)
    second_out = jnp.zeros_like(theta_out)
    for inner_step in range(STEPS):
        frame_rows = frames[0, inner_step]
        route_rows = routes[0, inner_step]
        gate_rows = gates[0, inner_step]
        slot_rows = slot_table(route_rows, experts)
        spread = jnp.broadcast_to(frame_rows[:, None, :], (tok_rows, 2, width))
        buffer = (
            jnp.zeros((experts, capacity, width), jnp.bfloat16)
            .at[route_rows, slot_rows]
            .set(spread)
        )
        first_w = theta_in[0].astype(jnp.bfloat16)
        second_w = theta_out[0].astype(jnp.bfloat16)
        received = lax.all_to_all(buffer, "exp", split_axis=0, concat_axis=0, tiled=True)
        expert_rows = received.reshape(-1, width)
        hidden = jnp.dot(expert_rows, first_w, preferred_element_type=jnp.float32)
        active = jax.nn.gelu(hidden).astype(jnp.bfloat16)
        produced = jnp.dot(active, second_w, preferred_element_type=jnp.float32).astype(
            jnp.bfloat16
        )
        returned = lax.all_to_all(
            produced.reshape(experts, capacity, width),
            "exp",
            split_axis=0,
            concat_axis=0,
            tiled=True,
        )
        picked = returned[route_rows, slot_rows].astype(jnp.float32)
        combined = jnp.sum(gate_rows[:, :, None] * picked, axis=1)
        residue = (combined - targets[0, inner_step].astype(jnp.float32)) / tok_rows
        cotangent = (gate_rows[:, :, None] * residue[:, None, :]).astype(jnp.bfloat16)
        cot_buffer = (
            jnp.zeros((experts, capacity, width), jnp.bfloat16)
            .at[route_rows, slot_rows]
            .set(cotangent)
        )
        cot_rows = lax.all_to_all(
            cot_buffer, "exp", split_axis=0, concat_axis=0, tiled=True
        ).reshape(-1, width)
        grad_out = contract_rows(active, cot_rows)[None]
        theta_out, first_out, second_out = adamw(
            theta_out, first_out, second_out, grad_out, inner_step + 1
        )
        upstream = lax.dot_general(
            cot_rows, second_w, (((1,), (1,)), ((), ())), preferred_element_type=jnp.float32
        )
        _, pull = jax.vjp(jax.nn.gelu, hidden)
        (local_grad,) = pull(upstream)
        dh_rows = local_grad.astype(jnp.bfloat16)
        grad_in = contract_rows(expert_rows, dh_rows)[None]
        theta_in, first_in, second_in = adamw(
            theta_in, first_in, second_in, grad_in, inner_step + 1
        )
    change_in = w_in.astype(jnp.float32) - theta_in
    change_out = w_out.astype(jnp.float32) - theta_out
    summed_in, summed_out = (
        lax.psum_scatter(
            change_in.astype(jnp.bfloat16), "rep", scatter_dimension=1, tiled=True
        ).astype(jnp.float32),
        lax.psum_scatter(
            change_out.astype(jnp.bfloat16), "rep", scatter_dimension=1, tiled=True
        ).astype(jnp.float32),
    )
    replicas = lax.axis_size("rep")
    part_in, new_mom_in = outer_update(w_in, mom_in, summed_in, replicas)
    part_out, new_mom_out = outer_update(w_out, mom_out, summed_out, replicas)
    new_w_in, new_w_out = (
        lax.all_gather(part_in, "rep", axis=1, tiled=True),
        lax.all_gather(part_out, "rep", axis=1, tiled=True),
    )
    return (new_w_in, new_w_out, new_mom_in, new_mom_out)


def solution(mesh):
    in_specs = (
        P("exp", None, None),
        P("exp", None, None),
        P("exp", "rep", None),
        P("exp", "rep", None),
        P("rep", None, "exp", None),
        P("rep", None, "exp", None),
        P("rep", None, "exp", None),
        P("rep", None, "exp", None),
    )
    out_specs = (
        P("exp", None, None),
        P("exp", None, None),
        P("exp", "rep", None),
        P("exp", "rep", None),
    )
    return jax.shard_map(
        per_device, mesh=mesh, in_specs=in_specs, out_specs=out_specs, check_vma=False
    )
```

profile of v0, /device:TPU:8, one launch (start us, length us, event | category | flops | bytes accessed | tf_op | source)
XLA Modules:
  0.0 653.4 jit_solution(5849435738672530555)
XLA Ops:
  7.2 0.7 fusion.111
  8.0 0.1 eq.54
  8.1 0.1 eq.50
  8.3 0.6 reduce-window.14
  8.9 0.2 slice_reduce_fusion.1
  9.2 0.1 add.168
  9.3 0.1 sub.55
  9.5 0.1 reshape.272
  9.7 1.1 slice_bitcast_fusion
  10.7 0.2 broadcast_in_dim.9
  10.9 0.1 reshape.274
  11.2 15.1 %scatter_fusion = bf16[16,32,768]{2,1,0:T(8,128)(2,1)S(1)} fusion(bf16[16,32,768]{2,1,0:T(8,128)(2,1)S(1)} %broadcast.227.clone, s32[256]{0:T(256)S(1)} %reshape.272, bf16[256,768]{1,0:T(8,128)(2,1)S(1)} %reshape.274), kind=kCustom, calls=%fused_computation.2 | custom fusion | bytes 1181696 | tf_op jit(solution)/shard_map/scatter | solution.py:58
  26.3 33.9 %all_to_all.30 = bf16[16,32,768]{2,1,0:T(8,128)(2,1)S(1)} all-to-all(bf16[16,32,768]{2,1,0:T(8,128)(2,1)S(1)} %scatter_fusion), channel_id=1, replica_groups=mesh['rep'=16,'exp'=16] {'exp'}, dimensions={0} | all-to-all | bytes 1572864 | tf_op jit(solution)/shard_map/all_to_all | solution.py:62
  60.2 3.2 fusion.52
  63.4 2.8 fusion.73
  66.3 3.5 all-to-all-start.1
  69.8 0.1 reshape.260
  70.1 22.9 %all-to-all-done.1 = bf16[16,32,768]{2,1,0:T(8,128)(2,1)S(1)} async-done(((bf16[16,32,768]{2,1,0:T(8,128)(2,1)}), bf16[16,32,768]{2,1,0:T(8,128)(2,1)S(1)}, u32[]{:S(2)}, u32[]{:S(2)}) %all-to-all-start.1) | async-done | bytes 786464 | tf_op jit(solution)/shard_map/all_to_all | solution.py:69
  93.0 2.4 gather_fusion
  95.4 0.4 reshape.296
  95.8 1.0 multiply_reduce_fusion.1
  96.9 0.4 multiply_convert_fusion.3
  97.3 0.1 reshape.280
  97.4 1.0 broadcast.227.clone.1
  98.4 34.6 %scatter_fusion.1 = bf16[16,32,768]{2,1,0:T(8,128)(2,1)} fusion(bf16[16,32,768]{2,1,0:T(8,128)(2,1)} %broadcast.227.clone.1, s32[256]{0:T(256)S(1)} %reshape.272, bf16[256,768]{1,0:T(8,128)(2,1)S(1)} %reshape.280), kind=kCustom, calls=%fused_computation.3 | custom fusion | bytes 1181696 | tf_op jit(solution)/shard_map/scatter | solution.py:83
  133.0 3.5 all-to-all-start.2
  136.6 0.1 eq.62
  136.7 0.1 eq.58
  136.9 0.6 reduce-window.16
  137.5 0.2 slice_reduce_fusion
  137.8 0.1 add.175
  138.1 0.1 reshape.284
  138.3 0.2 broadcast_in_dim.11
  138.5 0.1 reshape.286
  138.6 1.0 broadcast.227.clone.2
  139.6 34.6 %scatter_fusion.2 = bf16[16,32,768]{2,1,0:T(8,128)(2,1)} fusion(bf16[16,32,768]{2,1,0:T(8,128)(2,1)} %broadcast.227.clone.2, s32[256]{0:T(256)S(1)} %reshape.284, bf16[256,768]{1,0:T(8,128)(2,1)S(1)} %reshape.286), kind=kCustom, calls=%fused_computation.4 | custom fusion | bytes 1181696 | tf_op jit(solution)/shard_map/scatter | solution.py:58
  174.2 9.8 %all-to-all-start.3 = ((bf16[16,32,768]{2,1,0:T(8,128)(2,1)}), bf16[16,32,768]{2,1,0:T(8,128)(2,1)S(1)}, u32[]{:S(2)}, u32[]{:S(2)}) async-start(bf16[16,32,768]{2,1,0:T(8,128)(2,1)} %scatter_fusion.2), calls=%async_computation.3 | async-start | bytes 1572864 | tf_op jit(solution)/shard_map/all_to_all | solution.py:62
  184.0 8.3 %fusion.59 = f32[768,1536]{1,0:T(8,128)} fusion(bf16[512,768]{1,0:T(8,128)(2,1)S(1)} %bitcast.152, f32[512,1536]{1,0:T(8,128)} %copy-done.7, bf16[512,768]{1,0:T(8,128)(2,1)S(1)} %bitcast.155, bf16[1,1536,768]{2,1,0:T(8,128)(2,1)} %param.9), kind=kOutput, calls=%fused_computation.74 | convolution fusion | flops 2431647744 | bytes 11796480 | tf_op jit(solution)/shard_map/dot_general | solution.py:24
  192.2 10.0 %fusion.57 = (bf16[1,1536,768]{2,1,0:T(8,128)(2,1)}, f32[1536,768]{1,0:T(8,128)}) fusion(bf16[1,1536,768]{2,1,0:T(8,128)(2,1)} %param.9, bf16[512,768]{1,0:T(8,128)(2,1)S(1)} %bitcast.156, f32[512,1536]{1,0:T(8,128)} %copy-done.7), kind=kOutput, calls=%fused_computation.73 | convolution fusion | flops 1228013568 | bytes 13369344 | tf_op jit(solution)/shard_map/dot_general | solution.py:24
  202.2 5.1 all-to-all-done.3
  207.3 5.9 fusion.44
  213.2 2.8 fusion.76
  216.0 4.6 all-to-all-start.4
  220.7 0.2 reduce-scatter.5.cloned.1.call-start
  220.9 0.1 reshape.266
  221.1 23.0 %all-to-all-done.4 = bf16[16,32,768]{2,1,0:T(8,128)(2,1)S(1)} async-done(((bf16[16,32,768]{2,1,0:T(8,128)(2,1)}), bf16[16,32,768]{2,1,0:T(8,128)(2,1)S(1)}, u32[]{:S(2)}, u32[]{:S(2)}) %all-to-all-start.4) | async-done | bytes 786464 | tf_op jit(solution)/shard_map/all_to_all | solution.py:69
  244.1 2.4 gather_fusion.1
  246.5 0.4 reshape.297
  246.9 1.0 multiply_reduce_fusion
  248.0 0.4 multiply_convert_fusion.2
  248.3 0.1 reshape.292
  248.6 15.1 %scatter_fusion.3 = bf16[16,32,768]{2,1,0:T(8,128)(2,1)S(1)} fusion(bf16[16,32,768]{2,1,0:T(8,128)(2,1)S(1)} %broadcast.227, s32[256]{0:T(256)S(1)} %reshape.284, bf16[256,768]{1,0:T(8,128)(2,1)S(1)} %reshape.292), kind=kCustom, calls=%fused_computation.5 | custom fusion | bytes 1181696 | tf_op jit(solution)/shard_map/scatter | solution.py:83
  263.7 26.5 %all_to_all.31 = bf16[16,32,768]{2,1,0:T(8,128)(2,1)S(1)} all-to-all(bf16[16,32,768]{2,1,0:T(8,128)(2,1)S(1)} %scatter_fusion.3), channel_id=1, replica_groups=mesh['rep'=16,'exp'=16] {'exp'}, dimensions={0} | all-to-all | bytes 1572864 | tf_op jit(solution)/shard_map/all_to_all | solution.py:85
  290.2 11.3 %fusion.5 = bf16[1,1536,768]{2,1,0:T(8,128)(2,1)} fusion(bf16[1,1536,768]{2,1,0:T(8,128)(2,1)} %param.9, f32[1536,768]{1,0:T(8,128)} %get-tuple-element.23, bf16[512,768]{1,0:T(8,128)(2,1)S(1)} %bitcast.157, f32[512,1536]{1,0:T(8,128)} %copy-done.8), kind=kOutput, calls=%fused_computation.21 | convolution fusion | flops 1246887936 | bytes 13369344 | tf_op jit(solution)/shard_map/dot_general | solution.py:24
  301.6 0.3 reduce-scatter.3.cloned.1.call-start
  301.8 13.7 %fusion.2 = bf16[1,768,1536]{2,1,0:T(8,128)(2,1)} fusion(bf16[1,768,1536]{2,1,0:T(8,128)(2,1)} %param.8, f32[768,1536]{1,0:T(8,128)} %fusion.59, bf16[512,768]{1,0:T(8,128)(2,1)S(1)} %bitcast.154, f32[512,1536]{1,0:T(8,128)} %copy-done.8, bf16[512,768]{1,0:T(8,128)(2,1)S(1)} %bitcast.158, bf16[1,1536,768]{2,1,0:T(8,128)(2,1)} %get-tuple-element.22), kind=kOutput, calls=%fused_computation.18 | convolution fusion | flops 2463498240 | bytes 16515072 | tf_op jit(solution)/shard_map/dot_general | solution.py:24
  315.6 72.9 %reduce-scatter.5.cloned.1.call-done = bf16[1,96,768]{2,1,0:T(8,128)(2,1)} async-done(((bf16[1,1536,768]{2,1,0:T(8,128)(2,1)}), bf16[1,96,768]{2,1,0:T(8,128)(2,1)}) %reduce-scatter.5.cloned.1.call-update) | async-done | bytes 147472 | tf_op jit(solution)/shard_map/reduce_scatter | solution.py:108
  388.5 1.8 subtract_convert_fusion
  390.4 85.9 %reduce-scatter.3.cloned.1.call-done = bf16[1,48,1536]{2,1,0:T(8,128)(2,1)} async-done(((bf16[1,768,1536]{2,1,0:T(8,128)(2,1)}), bf16[1,48,1536]{2,1,0:T(8,128)(2,1)}) %reduce-scatter.3.cloned.1.call-update) | async-done | bytes 147472 | tf_op jit(solution)/shard_map/reduce_scatter | solution.py:105
  476.4 1.8 subtract_convert_fusion.1
  478.2 79.8 %all-gather.5.cloned.1.call-done = bf16[1,1536,768]{2,1,0:T(8,128)(2,1)} async-done(((bf16[1,96,768]{2,1,0:T(8,128)(2,1)}), bf16[1,1536,768]{2,1,0:T(8,128)(2,1)}) %all-gather.5.cloned.1.call-update) | async-done | bytes 2359312 | tf_op jit(solution)/shard_map/all_gather | solution.py:117
  558.0 84.1 %all-gather.3.cloned.1.call-done = bf16[1,768,1536]{2,1,0:T(8,128)(2,1)} async-done(((bf16[1,48,1536]{2,1,0:T(8,128)(2,1)}), bf16[1,768,1536]{2,1,0:T(8,128)(2,1)}) %all-gather.3.cloned.1.call-update) | async-done | bytes 2359312 | tf_op jit(solution)/shard_map/all_gather | solution.py:116
  642.1 3.2 copy.32
  645.3 1.4 copy.33
  (49 shorter events, 1.4 us)
Async XLA Ops:
  60.2 3.2 copy-start.5
  63.4 2.9 copy-start.7
  63.4 6.5 copy-start.6
  66.3 26.8 %all-to-all-start.1 = ((bf16[16,32,768]{2,1,0:T(8,128)(2,1)}), bf16[16,32,768]{2,1,0:T(8,128)(2,1)S(1)}, u32[]{:S(2)}, u32[]{:S(2)}) async-start(bf16[16,32,768]{2,1,0:T(8,128)(2,1)} %bitcast.7), calls=%async_computation.1 | async-start | bytes 1572864 | tf_op jit(solution)/shard_map/all_to_all | solution.py:69
  69.8 27.1 %copy-start.1 = (bf16[1,2,128,768]{3,2,1,0:T(8,128)(2,1)S(1)}, bf16[1,2,128,768]{3,2,1,0:T(8,128)(2,1)}, u32[]{:S(2)}) copy-start(bf16[1,2,128,768]{3,2,1,0:T(8,128)(2,1)} %param.13) | copy-start | bytes 1179652
  133.0 41.2 %all-to-all-start.2 = ((bf16[16,32,768]{2,1,0:T(8,128)(2,1)}), bf16[16,32,768]{2,1,0:T(8,128)(2,1)S(1)}, u32[]{:S(2)}, u32[]{:S(2)}) async-start(bf16[16,32,768]{2,1,0:T(8,128)(2,1)} %scatter_fusion.1), calls=%async_computation.2 | async-start | bytes 1572864 | tf_op jit(solution)/shard_map/all_to_all | solution.py:85
  174.2 33.1 %all-to-all-start.3 = ((bf16[16,32,768]{2,1,0:T(8,128)(2,1)}), bf16[16,32,768]{2,1,0:T(8,128)(2,1)S(1)}, u32[]{:S(2)}, u32[]{:S(2)}) async-start(bf16[16,32,768]{2,1,0:T(8,128)(2,1)} %scatter_fusion.2), calls=%async_computation.3 | async-start | bytes 1572864 | tf_op jit(solution)/shard_map/all_to_all | solution.py:62
  207.3 5.9 copy-start.9
  213.2 2.9 copy-start.8
  216.0 28.0 %all-to-all-start.4 = ((bf16[16,32,768]{2,1,0:T(8,128)(2,1)}), bf16[16,32,768]{2,1,0:T(8,128)(2,1)S(1)}, u32[]{:S(2)}, u32[]{:S(2)}) async-start(bf16[16,32,768]{2,1,0:T(8,128)(2,1)} %bitcast.19), calls=%async_computation.4 | async-start | bytes 1572864 | tf_op jit(solution)/shard_map/all_to_all | solution.py:69
  220.6 27.3 %copy-start.2 = (bf16[1,2,128,768]{3,2,1,0:T(8,128)(2,1)S(1)}, bf16[1,2,128,768]{3,2,1,0:T(8,128)(2,1)}, u32[]{:S(2)}) copy-start(bf16[1,2,128,768]{3,2,1,0:T(8,128)(2,1)} %param.13) | copy-start | bytes 1179652
  220.7 167.9 %reduce-scatter.5.cloned.1.call-start = ((), (), s32[]{:S(2)}) async-start(), calls=%async_computation.10 | async-start | bytes 2506752 | tf_op jit(solution)/shard_map/reduce_scatter | solution.py:108
  301.6 86.9 %copy-start.3 = (f32[1,96,768]{2,1,0:T(8,128)S(1)}, f32[1,96,768]{2,1,0:T(8,128)}, u32[]{:S(2)}) copy-start(f32[1,96,768]{2,1,0:T(8,128)} %param.11) | copy-start | bytes 884740
  301.6 174.8 %reduce-scatter.3.cloned.1.call-start = ((), (), s32[]{:S(2)}) async-start(), calls=%async_computation.8 | async-start | bytes 2506752 | tf_op jit(solution)/shard_map/reduce_scatter | solution.py:105
  315.5 160.9 %copy-start.4 = (f32[1,48,1536]{2,1,0:T(8,128)S(1)}, f32[1,48,1536]{2,1,0:T(8,128)}, u32[]{:S(2)}) copy-start(f32[1,48,1536]{2,1,0:T(8,128)} %param.10) | copy-start | bytes 884740
  315.5 242.4 %all-gather.5.cloned.1.call-start = ((), (), s32[]{:S(2)}) async-start(), calls=%async_computation.11 | async-start | bytes 2506752 | tf_op jit(solution)/shard_map/all_gather | solution.py:117
  390.4 251.7 %all-gather.3.cloned.1.call-start = ((), (), s32[]{:S(2)}) async-start(), calls=%async_computation.9 | async-start | bytes 2506752 | tf_op jit(solution)/shard_map/all_gather | solution.py:116
  558.0 87.3 %copy-start = (bf16[1,1536,768]{2,1,0:T(8,128)(2,1)S(1)}, bf16[1,1536,768]{2,1,0:T(8,128)(2,1)}, u32[]{:S(2)}) copy-start(bf16[1,1536,768]{2,1,0:T(8,128)(2,1)} %all-gather.5.cloned.1.call-done) | copy-start | bytes 7077892
Sparse Core Ops, SparseCore 0:
  301.7 86.7 reduce-scatter.4
  391.6 84.7 reduce-scatter.2
  478.2 79.7 all-gather.4
  560.2 81.8 all-gather.2
where the time goes:
time: 665 us; the launch traced here: 653 us
  waiting for transfers between devices  374 us (56%)
  local copies, waits for them, and re-layouts  117 us (18%)
  blocking collectives  60.4 us (9%)
  matrix products  58 us (9%)
  starting transfers between devices  21.9 us (3%)
  between operations  14.4 us (2%)
  other arithmetic  8 us (1%)
    reduce_scatter x1, waiting for transfers between devices, per_device(): lax.psum_scatter(change_in.astype(jnp.bfloat16), 'rep', scatter_dimension...  85.9 us
    all_gather x1, waiting for transfers between devices, per_device(): lax.all_gather(part_in, 'rep', axis=1, tiled=True)  84.1 us
    all_gather x1, waiting for transfers between devices, per_device(): lax.all_gather(part_out, 'rep', axis=1, tiled=True)  79.8 us
    reduce_scatter x1, waiting for transfers between devices, per_device(): lax.psum_scatter(change_out.astype(jnp.bfloat16), 'rep', scatter_dimensio...  72.9 us
    scatter x2, local copies, waits for them, and re-layouts, per_device(): buffer = jnp.zeros((experts, capacity, width), jnp.bfloat16).at[route_row...  49.7 us
    scatter x2, local copies, waits for them, and re-layouts, per_device(): cot_buffer = jnp.zeros((experts, capacity, width), jnp.bfloat16).at[route...  49.7 us
    all_to_all x2, waiting for transfers between devices, per_device(): lax.all_to_all(produced.reshape(experts, capacity, width), 'exp', split_a...  45.9 us
    dot_general x4, matrix products, contract_rows(): lax.dot_general(left, right, (((0,), (0,)), ((), ())), preferred_element_...  43.3 us
  transfers between devices with their start and end apart: 8, of which 7 were waited for; matrix products, arithmetic and copies ran while one was open for 11% of the time, Pallas kernels for 0%

commit v1 on v0

v1 whole, which is shorter than its diff:
```python
import functools
import math

import jax
import jax.numpy as jnp
from jax import lax
from jax.experimental import pallas as pl
from jax.experimental.pallas import tpu as pltpu
from jax.sharding import PartitionSpec as P

F32 = jnp.float32
BF16 = jnp.bfloat16
MIB = 1 << 20
NX = 4
NZ = 4


def dot(left, right, on_left=1, on_right=0):
    return lax.dot_general(
        left, right, (((on_left,), (on_right,)), ((), ())), preferred_element_type=F32
    )


def places(routes, capacity):
    rows = routes.shape[0]
    first, second = routes[:, 0:1], routes[:, 1:2]
    lane = lax.broadcasted_iota(jnp.int32, (rows, 128), 1)
    names_first, names_second = lane == first, lane == second
    named = jnp.where(names_first | names_second, 1.0, 0.0).astype(BF16)
    earlier = lax.broadcasted_iota(jnp.int32, (rows, rows), 0) > lax.broadcasted_iota(
        jnp.int32, (rows, rows), 1
    )
    count = dot(jnp.where(earlier, 1.0, 0.0).astype(BF16), named)
    slot_first = jnp.sum(jnp.where(names_first, count, 0.0), axis=1, keepdims=True)
    slot_second = jnp.sum(jnp.where(names_second, count, 0.0), axis=1, keepdims=True)
    return (
        first * capacity + slot_first.astype(jnp.int32),
        second * capacity + slot_second.astype(jnp.int32),
    )


def one_hot(place, size):
    lane = lax.broadcasted_iota(jnp.int32, (place.shape[0], size), 1)
    return jnp.where(lane == place, 1.0, 0.0).astype(BF16)


def gelu_and_slope(x):
    c = math.sqrt(2.0 / math.pi)
    square = x * x
    bent = jnp.tanh(c * (x + 0.044715 * (square * x)))
    half = 0.5 * (1.0 + bent)
    slope = half + 0.5 * x * (1.0 - bent * bent) * (c * (1.0 + 3 * 0.044715 * square))
    return x * half, slope


def after_one(weight, grad):
    ratio = grad / (jnp.abs(grad) + 0.01)
    return weight - 0.004 * (ratio + 0.1 * weight)


def change_of_two(weight, grad_one, grad_two):
    theta = after_one(weight, grad_one)
    first = (0.09 / 0.19) * grad_one + (0.1 / 0.19) * grad_two
    second = (0.0475 / 0.0975) * (grad_one * grad_one) + (0.05 / 0.0975) * (grad_two * grad_two)
    ratio = first / (jnp.sqrt(second) + 0.01)
    return weight - (theta - 0.004 * (ratio + 0.1 * theta))


def params(limit=48):
    return pltpu.CompilerParams(vmem_limit_bytes=limit * MIB)


def cost(flops, size):
    return pl.CostEstimate(flops=int(flops), bytes_accessed=int(size), transcendentals=0)


def place_kernel(capacity, routes_ref, frames_ref, out_ref):
    size = out_ref.shape[0]
    first, second = places(routes_ref[...], capacity)
    spread = one_hot(first, size) + one_hot(second, size)
    out_ref[...] = dot(spread, frames_ref[...], 0, 0).astype(BF16)


def place_frames(routes, frames, size, capacity):
    return pl.pallas_call(
        functools.partial(place_kernel, capacity),
        out_shape=jax.ShapeDtypeStruct((size, frames.shape[1]), BF16),
        compiler_params=params(),
        cost_estimate=cost(2e8, 2e6),
        name="place_frames",
    )(routes, frames)


def residue_kernel(capacity, routes_ref, gates_ref, targets_ref, returned_ref, out_ref):
    size = out_ref.shape[0]
    rows = routes_ref.shape[0]
    first, second = places(routes_ref[...], capacity)
    hot_first, hot_second = one_hot(first, size), one_hot(second, size)
    gate_first, gate_second = gates_ref[:, 0:1], gates_ref[:, 1:2]
    returned = returned_ref[...]
    combined = gate_first * dot(hot_first, returned) + gate_second * dot(hot_second, returned)
    residue = (combined - targets_ref[...].astype(F32)) * (1.0 / rows)
    cot_first = (gate_first * residue).astype(BF16)
    cot_second = (gate_second * residue).astype(BF16)
    out_ref[...] = (dot(hot_first, cot_first, 0, 0) + dot(hot_second, cot_second, 0, 0)).astype(BF16)


def place_residue(routes, gates, targets, returned, capacity):
    return pl.pallas_call(
        functools.partial(residue_kernel, capacity),
        out_shape=jax.ShapeDtypeStruct(returned.shape, BF16),
        compiler_params=params(),
        cost_estimate=cost(4e8, 4e6),
        name="place_residue",
    )(routes, gates, targets, returned)


def forward_kernel(rows_ref, w_in_ref, w_out_ref, hidden_ref, active_ref, produced_ref, total):
    step = pl.program_id(0)
    hidden = dot(rows_ref[...], w_in_ref[...])
    hidden_ref[...] = hidden
    active = gelu_and_slope(hidden)[0].astype(BF16)
    active_ref[...] = active
    part = dot(active, w_out_ref[...])

    @pl.when(step == 0)
    def _():
        total[...] = part

    @pl.when(step > 0)
    def _():
        total[...] += part

    @pl.when(step == pl.num_programs(0) - 1)
    def _():
        produced_ref[...] = total[...].astype(BF16)


def forward(rows, w_in, w_out, tile=512):
    slots, width = rows.shape
    hid = w_in.shape[1]
    whole = pl.BlockSpec((slots, width), lambda i: (0, 0))
    by_col = pl.BlockSpec((slots, tile), lambda i: (0, i))
    return pl.pallas_call(
        forward_kernel,
        grid=(hid // tile,),
        in_specs=[
            whole,
            pl.BlockSpec((width, tile), lambda i: (0, i)),
            pl.BlockSpec((tile, width), lambda i: (i, 0)),
        ],
        out_specs=[by_col, by_col, whole],
        out_shape=[
            jax.ShapeDtypeStruct((slots, hid), F32),
            jax.ShapeDtypeStruct((slots, hid), BF16),
            jax.ShapeDtypeStruct((slots, width), BF16),
        ],
        scratch_shapes=[pltpu.VMEM((slots, width), F32)],
        compiler_params=params(),
        cost_estimate=cost(2.4e9, 1e7),
        name="forward",
    )(rows, w_in, w_out)


def turn_kernel(
    rows_ref,
    next_ref,
    cot_ref,
    w_in_ref,
    w_out_ref,
    hidden_ref,
    active_ref,
    dh_ref,
    theta_out_ref,
    hidden_next_ref,
    active_next_ref,
    produced_ref,
    total,
    turned,
):
    step = pl.program_id(0)

    @pl.when(step == 0)
    def _():
        turned[...] = rows_ref[...].T

    cot = cot_ref[...]
    w_out = w_out_ref[...]
    upstream = dot(cot, w_out, 1, 1)
    dh = (upstream * gelu_and_slope(hidden_ref[...])[1]).astype(BF16)
    dh_ref[...] = dh
    grad_in = dot(turned[...], dh)
    theta_in = after_one(w_in_ref[...].astype(F32), grad_in).astype(BF16)
    hidden = dot(next_ref[...], theta_in)
    hidden_next_ref[...] = hidden
    grad_out = dot(active_ref[...], cot, 0, 0)
    theta_out = after_one(w_out.astype(F32), grad_out).astype(BF16)
    theta_out_ref[...] = theta_out
    active = gelu_and_slope(hidden)[0].astype(BF16)
    active_next_ref[...] = active
    part = dot(active, theta_out)

    @pl.when(step == 0)
    def _():
        total[...] = part

    @pl.when(step > 0)
    def _():
        total[...] += part

    @pl.when(step == pl.num_programs(0) - 1)
    def _():
        produced_ref[...] = total[...].astype(BF16)


def turn(rows, next_rows, cot, w_in, w_out, hidden, active, tile=256):
    slots, width = rows.shape
    hid = w_in.shape[1]
    whole = pl.BlockSpec((slots, width), lambda i: (0, 0))
    by_col = pl.BlockSpec((slots, tile), lambda i: (0, i))
    by_row = pl.BlockSpec((tile, width), lambda i: (i, 0))
    return pl.pallas_call(
        turn_kernel,
        grid=(hid // tile,),
        in_specs=[
            whole,
            whole,
            whole,
            pl.BlockSpec((width, tile), lambda i: (0, i)),
            by_row,
            by_col,
            by_col,
        ],
        out_specs=[by_col, by_row, by_col, by_col, whole],
        out_shape=[
            jax.ShapeDtypeStruct((slots, hid), BF16),
            jax.ShapeDtypeStruct((hid, width), BF16),
            jax.ShapeDtypeStruct((slots, hid), F32),
            jax.ShapeDtypeStruct((slots, hid), BF16),
            jax.ShapeDtypeStruct((slots, width), BF16),
        ],
        scratch_shapes=[pltpu.VMEM((slots, width), F32), pltpu.VMEM((width, slots), BF16)],
        compiler_params=params(),
        cost_estimate=cost(7e9, 2e7),
        name="turn",
    )(rows, next_rows, cot, w_in, w_out, hidden, active)


PARTS = {
    0: (("own", 0), ("own", 2)),
    1: (("far_plus", 2), ("near_plus", 0)),
    2: (("far_minus", 0), ("far_plus", 0)),
    3: (("near_minus", 0), ("far_minus", 2)),
}
PART_SHARDS = {"far_minus": 4, "far_plus": 4, "near_minus": 2, "near_plus": 2, "own": 4}
HALVES = ((1, 3), (0, 2))


def store_change(rep, band, w_ref, grad_one, grad_two, outs):
    x, z = rep % NX, rep // NX
    for k in range(NX):
        for half, members in enumerate(HALVES):
            name, at = PARTS[k][half]
            for i, m in enumerate(members):
                first = pl.multiple_of((jnp.bitwise_xor(z, m) * NX + (x + k) % NX) * band, 16)
                rows = pl.ds(first, band)
                change = change_of_two(w_ref[rows, :].astype(F32), grad_one[rows, :], grad_two[rows, :])
                outs[name][at + i] = change.astype(BF16)


def change_out_kernel(rep_ref, w_ref, act_one, cot_one, act_two, cot_two, *rest):
    outs = dict(zip(PART_SHARDS, rest[:5]))
    grad_one, grad_two = rest[5:]
    grad_one[...] = dot(act_one[...], cot_one[...], 0, 0)
    grad_two[...] = dot(act_two[...], cot_two[...], 0, 0)
    band = outs["own"].shape[1]
    store_change(rep_ref[0], band, w_ref, grad_one, grad_two, outs)


def change_out(rep, replicas, w_out, act_one, cot_one, act_two, cot_two, tile=256):
    slots, hid = act_one.shape
    width = cot_one.shape[1]
    band = hid // replicas
    act = pl.BlockSpec((slots, hid), lambda i: (0, 0))
    cot = pl.BlockSpec((slots, tile), lambda i: (0, i))
    return pl.pallas_call(
        change_out_kernel,
        grid=(width // tile,),
        in_specs=[
            pl.BlockSpec(memory_space=pltpu.SMEM),
            pl.BlockSpec((hid, tile), lambda i: (0, i)),
            act,
            cot,
            act,
            cot,
        ],
        out_specs=[pl.BlockSpec((n, band, tile), lambda i: (0, 0, i)) for n in PART_SHARDS.values()],
        out_shape=[jax.ShapeDtypeStruct((n, band, width), BF16) for n in PART_SHARDS.values()],
        scratch_shapes=[pltpu.VMEM((hid, tile), F32), pltpu.VMEM((hid, tile), F32)],
        compiler_params=params(),
        cost_estimate=cost(2.4e9, 1e7),
        name="change_out",
    )(rep, w_out, act_one, cot_one, act_two, cot_two)


def change_in_kernel(
    rep_ref, w_ref, rows_one, dh_one, rows_two, cot_two, theta_out, hidden_two, *rest
):
    outs = dict(zip(PART_SHARDS, rest[:5]))
    grad_one, grad_two, turned_one, turned_two = rest[5:]

    @pl.when(pl.program_id(0) == 0)
    def _():
        turned_one[...] = rows_one[...].T
        turned_two[...] = rows_two[...].T

    upstream = dot(cot_two[...], theta_out[...], 1, 1)
    dh_two = (upstream * gelu_and_slope(hidden_two[...])[1]).astype(BF16)
    grad_one[...] = dot(turned_one[...], dh_one[...])
    grad_two[...] = dot(turned_two[...], dh_two)
    band = outs["own"].shape[1]
    store_change(rep_ref[0], band, w_ref, grad_one, grad_two, outs)


def change_in(rep, replicas, w_in, rows_one, dh_one, rows_two, cot_two, theta_out, hidden_two, tile=256):
    slots, hid = dh_one.shape
    width = rows_one.shape[1]
    band = width // replicas
    whole = pl.BlockSpec((slots, width), lambda i: (0, 0))
    by_col = pl.BlockSpec((slots, tile), lambda i: (0, i))
    return pl.pallas_call(
        change_in_kernel,
        grid=(hid // tile,),
        in_specs=[
            pl.BlockSpec(memory_space=pltpu.SMEM),
            pl.BlockSpec((width, tile), lambda i: (0, i)),
            whole,
            by_col,
            whole,
            whole,
            pl.BlockSpec((tile, width), lambda i: (i, 0)),
            by_col,
        ],
        out_specs=[pl.BlockSpec((n, band, tile), lambda i: (0, 0, i)) for n in PART_SHARDS.values()],
        out_shape=[jax.ShapeDtypeStruct((n, band, hid), BF16) for n in PART_SHARDS.values()],
        scratch_shapes=[
            pltpu.VMEM((width, tile), F32),
            pltpu.VMEM((width, tile), F32),
            pltpu.VMEM((width, slots), BF16),
            pltpu.VMEM((width, slots), BF16),
        ],
        compiler_params=params(),
        cost_estimate=cost(3.6e9, 1.5e7),
        name="change_in",
    )(rep, w_in, rows_one, dh_one, rows_two, cot_two, theta_out, hidden_two)


def rep_permutation(step_x, flip_z):
    pairs = []
    for z in range(NZ):
        for x in range(NX):
            pairs.append((z * NX + x, (z ^ flip_z) * NX + (x + step_x) % NX))
    return pairs


def shift_x(array, step):
    return lax.ppermute(array, "rep", rep_permutation(step, 0))


def swap_z(array, flip):
    return lax.ppermute(array, "rep", rep_permutation(0, flip))


def add(*terms):
    return sum(term.astype(F32) for term in terms)


def reduce_to_owner(parts):
    far_minus, far_plus, near_minus, near_plus, own = parts
    from_plus = shift_x(far_minus, -1)
    from_minus = shift_x(far_plus, 1)
    last_plus = shift_x(add(near_minus, from_plus[:2]).astype(BF16), -1)
    last_minus = shift_x(add(near_plus, from_minus[:2]).astype(BF16), 1)
    half_a = add(own[:2], from_minus[2:], last_plus).astype(BF16)
    other = swap_z(half_a, 1)
    half_b = add(own[2:], from_plus[2:], last_minus)
    mine = half_b + other.astype(F32)
    across = swap_z(mine[1].astype(BF16), 2)
    return mine[0] + across.astype(F32)


def assemble_kernel(rep_ref, home, plus, minus, cross_a, cross_b, out, sem):
    x, z = rep_ref[0] % NX, rep_ref[0] // NX
    band = home.shape[1]
    copies = []
    for k, source in ((0, home), (1, plus), (3, minus), (2, None)):
        for m in range(NZ):
            if source is None:
                half = cross_a if m < 2 else cross_b
                block = half.at[m % 2]
            else:
                block = source.at[m]
            first = pl.multiple_of((jnp.bitwise_xor(z, m) * NX + (x + k) % NX) * band, 16)
            copies.append(pltpu.make_async_copy(block, out.at[pl.ds(first, band), :], sem.at[len(copies)]))
    for copy in copies:
        copy.start()
    for copy in copies:
        copy.wait()


def gather_from_owner(rep, own):
    band, columns = own.shape
    pair = jnp.stack([own, swap_z(own, 2)])
    other = swap_z(pair, 1)
    home = jnp.stack([pair[0], other[0], pair[1], other[1]])
    minus = shift_x(home, 1)
    plus = shift_x(home, -1)
    cross_a = shift_x(minus[:2], 1)
    cross_b = shift_x(plus[2:], -1)
    any_spec = pl.BlockSpec(memory_space=pl.ANY)
    return pl.pallas_call(
        assemble_kernel,
        in_specs=[pl.BlockSpec(memory_space=pltpu.SMEM)] + [any_spec] * 5,
        out_specs=any_spec,
        out_shape=jax.ShapeDtypeStruct((NZ * NX * band, columns), BF16),
        scratch_shapes=[pltpu.SemaphoreType.DMA((NZ * NX,))],
        cost_estimate=cost(0, 5e6),
        name="assemble",
    )(rep, home, plus, minus, cross_a, cross_b)


def outer_update(rep, start_w, momentum, summed, replicas):
    averaged = summed / replicas
    new_momentum = 0.9 * momentum + averaged
    rows = momentum.shape[0]
    own_rows = lax.dynamic_slice_in_dim(start_w, rep * rows, rows, 0).astype(F32)
    return (own_rows - 0.7 * (averaged + 0.9 * new_momentum)).astype(BF16), new_momentum


def exchange(rows, experts):
    slots, width = rows.shape
    block = rows.reshape(experts, slots // experts, width)
    return lax.all_to_all(block, "exp", split_axis=0, concat_axis=0, tiled=True).reshape(slots, width)


def per_device(w_in, w_out, mom_in, mom_out, frames, targets, routes, gates):
    experts = lax.axis_size("exp")
    replicas = lax.axis_size("rep")
    rep = lax.axis_index("rep")
    rep_ref = rep.reshape(1).astype(jnp.int32)
    capacity = 4 * frames.shape[2] // experts
    slots = experts * capacity
    w_in, w_out, mom_in, mom_out = w_in[0], w_out[0], mom_in[0], mom_out[0]
    frames, targets, routes, gates = frames[0], targets[0], routes[0], gates[0]

    rows_one = exchange(place_frames(routes[0], frames[0], slots, capacity), experts)
    hidden_one, active_one, produced = forward(rows_one, w_in, w_out)
    rows_two = exchange(place_frames(routes[1], frames[1], slots, capacity), experts)
    returned = exchange(produced, experts)
    cot_one = exchange(place_residue(routes[0], gates[0], targets[0], returned, capacity), experts)
    dh_one, theta_out, hidden_two, active_two, produced = turn(
        rows_one, rows_two, cot_one, w_in, w_out, hidden_one, active_one
    )
    returned = exchange(produced, experts)
    cot_two = exchange(place_residue(routes[1], gates[1], targets[1], returned, capacity), experts)

    parts_out = change_out(rep_ref, replicas, w_out, active_one, cot_one, active_two, cot_two)
    parts_in = change_in(
        rep_ref, replicas, w_in, rows_one, dh_one, rows_two, cot_two, theta_out, hidden_two
    )
    summed_out = reduce_to_owner(parts_out)
    summed_in = reduce_to_owner(parts_in)
    part_out, new_mom_out = outer_update(rep, w_out, mom_out, summed_out, replicas)
    new_w_out = gather_from_owner(rep_ref, part_out)
    part_in, new_mom_in = outer_update(rep, w_in, mom_in, summed_in, replicas)
    new_w_in = gather_from_owner(rep_ref, part_in)
    return (new_w_in[None], new_w_out[None], new_mom_in[None], new_mom_out[None])


def solution(mesh):
    in_specs = (
        P("exp", None, None),
        P("exp", None, None),
        P("exp", "rep", None),
        P("exp", "rep", None),
        P("rep", None, "exp", None),
        P("rep", None, "exp", None),
        P("rep", None, "exp", None),
        P("rep", None, "exp", None),
    )
    out_specs = (
        P("exp", None, None),
        P("exp", None, None),
        P("exp", "rep", None),
        P("exp", "rep", None),
    )
    return jax.shard_map(
        per_device, mesh=mesh, in_specs=in_specs, out_specs=out_specs, check_vma=False
    )
```

time: 665 us -> 485 us (0.73); the launches traced: 653 us -> 481 us
  waiting for transfers between devices: 374 us -> 139 us
  Pallas kernels: 0 us -> 198 us
  local copies, waits for them, and re-layouts: 117 us -> 9.57 us
  matrix products: 58 us -> 0 us
  starting transfers between devices: 21.9 us -> 65.1 us
  between operations: 14.4 us -> 1.16 us
    pallas_call x0 -> x10, Pallas kernels: none -> 198 us  [the longest x2 145 us: gather_from_owner(): pl.pallas_call(assemble_kernel, in_specs=[pl.BlockSpec(memory_space=pltpu...]
    all_gather x2 -> x0, waiting for transfers between devices: 164 us -> none  [the longest x1 84.1 us: per_device(): lax.all_gather(part_in, 'rep', axis=1, tiled=True)]
    reduce_scatter x2 -> x0, waiting for transfers between devices: 159 us -> none  [the longest x1 85.9 us: per_device(): lax.psum_scatter(change_in.astype(jnp.bfloat16), 'rep', scatter_dimension...]
    scatter x4 -> x0, local copies, waits for them, and re-layouts: 99.4 us -> none  [the longest x2 49.7 us: per_device(): buffer = jnp.zeros((experts, capacity, width), jnp.bfloat16).at[route_row...]
    dot_general x8 -> x0, matrix products: 58 us -> none  [the longest x4 43.3 us: contract_rows(): lax.dot_general(left, right, (((0,), (0,)), ((), ())), preferred_element_...]
    ppermute x0 -> x24, starting transfers between devices: none -> 50.8 us  [the longest x16 25.4 us: shift_x(): return lax.ppermute(array, 'rep', rep_permutation(step, 0))]
    ppermute x0 -> x24, waiting for transfers between devices: none -> 49.1 us  [the longest x16 27.1 us: shift_x(): return lax.ppermute(array, 'rep', rep_permutation(step, 0))]
    all_to_all x4, waiting for transfers between devices: 51 us -> 89.5 us  [exchange(): lax.all_to_all(block, 'exp', split_axis=0, concat_axis=0, tiled=True)]
  transfers between devices with their start and end apart: 8 -> 28, of which waited for: 7 -> 16; matrix products, arithmetic and copies ran while one was open for 11% -> 2% of each run, Pallas kernels for 0% -> 18%
where the time goes in v1:
time: 485 us; the launch traced here: 481 us
  Pallas kernels  198 us (41%)
  waiting for transfers between devices  139 us (29%)
  starting transfers between devices  65.1 us (13%)
  blocking collectives  60.4 us (12%)
  local copies, waits for them, and re-layouts  9.57 us (2%)
  other arithmetic  8.24 us (2%)
    pallas_call x2, Pallas kernels, gather_from_owner(): pl.pallas_call(assemble_kernel, in_specs=[pl.BlockSpec(memory_space=pltpu...  145 us
    all_to_all x4, waiting for transfers between devices, exchange(): lax.all_to_all(block, 'exp', split_axis=0, concat_axis=0, tiled=True)  89.5 us
    all_to_all x2, blocking collectives, exchange(): lax.all_to_all(block, 'exp', split_axis=0, concat_axis=0, tiled=True)  60.4 us
    ppermute x16, waiting for transfers between devices, shift_x(): return lax.ppermute(array, 'rep', rep_permutation(step, 0))  27.1 us
    ppermute x16, starting transfers between devices, shift_x(): return lax.ppermute(array, 'rep', rep_permutation(step, 0))  25.4 us
    ppermute x8, starting transfers between devices, swap_z(): return lax.ppermute(array, 'rep', rep_permutation(0, flip))  25.4 us
    ppermute x8, waiting for transfers between devices, swap_z(): return lax.ppermute(array, 'rep', rep_permutation(0, flip))  22 us
    pallas_call x1, Pallas kernels, turn(): pl.pallas_call(turn_kernel, grid=(hid // tile,), in_specs=[whole, whole,...  15.7 us
  transfers between devices with their start and end apart: 28, of which 16 were waited for; matrix products, arithmetic and copies ran while one was open for 2% of the time, Pallas kernels for 18%

profile of v1, /device:TPU:8, one launch (start us, length us, event | category | flops | bytes accessed | tf_op | source)
XLA Modules:
  0.0 481.0 jit_solution(9172063009154577129)
XLA Ops:
  0.6 0.7 fusion.13
  1.4 1.2 slice_bitcast_fusion.4
  2.7 0.8 place_frames.2
  3.5 33.9 %all_to_all.30 = bf16[16,32,768]{2,1,0:T(8,128)(2,1)S(1)} all-to-all(bf16[16,32,768]{2,1,0:T(8,128)(2,1)S(1)} %bitcast.79), channel_id=1, replica_groups=mesh['rep'=16,'exp'=16] {'exp'}, dimensions={0} | all-to-all | bytes 1572864 | tf_op jit(solution)/shard_map/all_to_all | solution.py:443
  37.4 6.6 %forward.1 = (f32[512,1536]{1,0:T(8,128)}, bf16[512,1536]{1,0:T(8,128)(2,1)S(1)}, bf16[512,768]{1,0:T(8,128)(2,1)}) custom-call(bf16[512,768]{1,0:T(8,128)(2,1)S(1)} %bitcast.83, bf16[768,1536]{1,0:T(8,128)(2,1)S(1)} %bitcast.101, bf16[1536,768]{1,0:T(8,128)(2,1)} %bitcast.112), custom_call_target="tpu_custom_call" | custom-call | flops 2400000000 | bytes 10000000 | tf_op jit(solution)/shard_map/forward/pallas_call | solution.py:144
  44.0 1.1 copy-done.10
  45.2 3.6 all-to-all-start.2
  48.9 1.7 place_frames.3
  50.6 21.4 %all-to-all-done.2 = bf16[16,32,768]{2,1,0:T(8,128)(2,1)S(1)} async-done(((bf16[16,32,768]{2,1,0:T(8,128)(2,1)}), bf16[16,32,768]{2,1,0:T(8,128)(2,1)S(1)}, u32[]{:S(2)}, u32[]{:S(2)}) %all-to-all-start.2) | async-done | bytes 786464 | tf_op jit(solution)/shard_map/all_to_all | solution.py:443
  72.0 3.5 all-to-all-start.1
  75.7 1.3 place_residue.2
  77.0 21.8 %all-to-all-done.1 = bf16[16,32,768]{2,1,0:T(8,128)(2,1)S(1)} async-done(((bf16[16,32,768]{2,1,0:T(8,128)(2,1)}), bf16[16,32,768]{2,1,0:T(8,128)(2,1)S(1)}, u32[]{:S(2)}, u32[]{:S(2)}) %all-to-all-start.1) | async-done | bytes 786464 | tf_op jit(solution)/shard_map/all_to_all | solution.py:443
  98.8 26.5 %all_to_all.31 = bf16[16,32,768]{2,1,0:T(8,128)(2,1)S(1)} all-to-all(bf16[16,32,768]{2,1,0:T(8,128)(2,1)S(1)} %bitcast.82), channel_id=1, replica_groups=mesh['rep'=16,'exp'=16] {'exp'}, dimensions={0} | all-to-all | bytes 1572864 | tf_op jit(solution)/shard_map/all_to_all | solution.py:443
  125.3 15.7 %turn.1 = (bf16[512,1536]{1,0:T(8,128)(2,1)S(1)}, bf16[1536,768]{1,0:T(8,128)(2,1)}, f32[512,1536]{1,0:T(8,128)}, bf16[512,1536]{1,0:T(8,128)(2,1)}, bf16[512,768]{1,0:T(8,128)(2,1)S(1)}) custom-call(bf16[512,768]{1,0:T(8,128)(2,1)S(1)} %bitcast.84, bf16[512,768]{1,0:T(8,128)(2,1)S(1)} %bitcast.86, bf16[512,768]{1,0:T(8,128)(2,1)S(1)} %bitcast.88, ...), custom_call_target="tpu_custom_call" | custom-call | flops 7000000000 | bytes 20000000 | tf_op jit(solution)/shard_map/turn/pallas_call | solution.py:222
  141.1 0.9 copy-done.2
  142.0 1.2 copy-done.9
  143.1 3.6 all-to-all-start.4
  146.9 23.1 %all-to-all-done.4 = bf16[16,32,768]{2,1,0:T(8,128)(2,1)S(1)} async-done(((bf16[16,32,768]{2,1,0:T(8,128)(2,1)}), bf16[16,32,768]{2,1,0:T(8,128)(2,1)S(1)}, u32[]{:S(2)}, u32[]{:S(2)}) %all-to-all-start.4) | async-done | bytes 786464 | tf_op jit(solution)/shard_map/all_to_all | solution.py:443
  170.0 2.2 place_residue.3
  172.2 3.5 all-to-all-start.5
  175.7 23.2 %all-to-all-done.5 = bf16[16,32,768]{2,1,0:T(8,128)(2,1)S(1)} async-done(((bf16[16,32,768]{2,1,0:T(8,128)(2,1)}), bf16[16,32,768]{2,1,0:T(8,128)(2,1)S(1)}, u32[]{:S(2)}, u32[]{:S(2)}) %all-to-all-start.5) | async-done | bytes 786464 | tf_op jit(solution)/shard_map/all_to_all | solution.py:443
  199.0 1.4 copy-done.11
  200.4 11.2 %change_out.1 = (bf16[4,96,768]{2,1,0:T(8,128)(2,1)S(1)}, bf16[4,96,768]{2,1,0:T(8,128)(2,1)}, bf16[2,96,768]{2,1,0:T(8,128)(2,1)S(1)}, bf16[2,96,768]{2,1,0:T(8,128)(2,1)S(1)}, bf16[4,96,768]{2,1,0:T(8,128)(2,1)S(1)}) custom-call(s32[1]{0:T(128)} %bitcast.rep_ref, bf16[1536,768]{1,0:T(8,128)(2,1)} %bitcast.114, bf16[512,1536]{1,0:T(8,128)(2,1)S(1)} %copy-done.11, ...), custom_call_target="tpu_custom_call" | custom-call | flops 2400000000 | bytes 10000000 | tf_op jit(solution)/shard_map/change_out/pallas_call | solution.py:286
  211.6 2.8 collective-permute-start.12
  214.4 12.8 %change_in.1 = (bf16[4,48,1536]{2,1,0:T(8,128)(2,1)S(1)}, bf16[4,48,1536]{2,1,0:T(8,128)(2,1)}, bf16[2,48,1536]{2,1,0:T(8,128)(2,1)S(1)}, bf16[2,48,1536]{2,1,0:T(8,128)(2,1)S(1)}, bf16[4,48,1536]{2,1,0:T(8,128)(2,1)S(1)}) custom-call(s32[1]{0:T(128)} %bitcast.rep_ref, bf16[768,1536]{1,0:T(8,128)(2,1)} %bitcast.100, bf16[512,768]{1,0:T(8,128)(2,1)S(1)} %bitcast.85, ...), custom_call_target="tpu_custom_call" | custom-call | flops 3600000000 | bytes 15000000 | tf_op jit(solution)/shard_map/change_in/pallas_call | solution.py:331
  227.2 0.8 copy-done.3
  228.0 0.8 collective-permute-start
  228.8 1.3 collective-permute-start.13
  230.1 0.9 add_convert_fusion.1
  231.0 3.2 collective-permute-start.15
  234.2 6.9 %collective-permute-done = bf16[4,48,1536]{2,1,0:T(8,128)(2,1)S(1)} collective-permute-done((bf16[4,48,1536]{2,1,0:T(8,128)(2,1)S(1)}, bf16[4,48,1536]{2,1,0:T(8,128)(2,1)S(1)}, u32[]{:S(2)}, u32[]{:S(2)}) %collective-permute-start) | collective-permute-done | bytes 589856 | tf_op jit(solution)/shard_map/ppermute | solution.py:367
  241.1 0.8 add_convert_fusion.4
  241.9 3.4 collective-permute-start.3
  245.2 0.5 collective-permute-done.13
  245.8 1.5 add_convert_fusion.2
  247.4 6.8 %collective-permute-start.16 = (bf16[2,96,768]{2,1,0:T(8,128)(2,1)S(1)}, bf16[2,96,768]{2,1,0:T(8,128)(2,1)S(1)}, u32[]{:S(2)}, u32[]{:S(2)}) collective-permute-start(bf16[2,96,768]{2,1,0:T(8,128)(2,1)S(1)} %get-tuple-element.45), channel_id=1, source_target_pairs={{0,64},{16,80},{32,96},{48,112},{64,0},{80,16},{96,32},{112,48},{1... | collective-permute-start | bytes 884744 | tf_op jit(solution)/shard_map/ppermute | solution.py:371
  254.2 1.1 add_convert_fusion.5
  255.3 0.7 collective-permute-start.2
  256.1 6.2 %collective-permute-start.4 = (bf16[2,48,1536]{2,1,0:T(8,128)(2,1)S(1)}, bf16[2,48,1536]{2,1,0:T(8,128)(2,1)S(1)}, u32[]{:S(2)}, u32[]{:S(2)}) collective-permute-start(bf16[2,48,1536]{2,1,0:T(8,128)(2,1)S(1)} %get-tuple-element.47), channel_id=1, source_target_pairs={{0,64},{16,80},{32,96},{48,112},{64,0},{80,16},{96,32},{112,48},{1... | collective-permute-start | bytes 884744 | tf_op jit(solution)/shard_map/ppermute | solution.py:371
  262.5 5.5 %collective-permute-start.17 = (bf16[96,768]{1,0:T(8,128)(2,1)S(1)}, bf16[96,768]{1,0:T(8,128)(2,1)S(1)}, u32[]{:S(2)}, u32[]{:S(2)}) collective-permute-start(bf16[96,768]{1,0:T(8,128)(2,1)S(1)} %fusion.9), channel_id=1, source_target_pairs={{0,128},{16,144},{32,160},{48,176},{64,192},{80,208},{96,224},{112... | collective-permute-start | bytes 442376 | tf_op jit(solution)/shard_map/ppermute | solution.py:371
  268.0 0.6 collective-permute-done.4
  268.8 4.0 collective-permute-start.5
  272.8 0.6 collective-permute-done.17
  273.4 1.7 fusion.7
  275.1 0.8 collective-permute-start.18
  275.9 7.6 %collective-permute-done.5 = bf16[48,1536]{1,0:T(8,128)(2,1)S(1)} collective-permute-done((bf16[48,1536]{1,0:T(8,128)(2,1)S(1)}, bf16[48,1536]{1,0:T(8,128)(2,1)S(1)}, u32[]{:S(2)}, u32[]{:S(2)}) %collective-permute-start.5) | collective-permute-done | bytes 147488 | tf_op jit(solution)/shard_map/ppermute | solution.py:371
  283.4 1.7 fusion.6
  285.2 0.8 collective-permute-done.18
  286.0 2.0 collective-permute-start.19
  288.0 5.1 %collective-permute-done.6 = bf16[48,1536]{1,0:T(8,128)(2,1)S(1)} collective-permute-done((bf16[48,1536]{1,0:T(8,128)(2,1)S(1)}, bf16[48,1536]{1,0:T(8,128)(2,1)S(1)}, u32[]{:S(2)}, u32[]{:S(2)}) %collective-permute-start.6) | collective-permute-done | bytes 147488 | tf_op jit(solution)/shard_map/ppermute | solution.py:371
  293.2 5.3 %collective-permute-done.19 = bf16[2,96,768]{2,1,0:T(8,128)(2,1)S(1)} collective-permute-done((bf16[2,96,768]{2,1,0:T(8,128)(2,1)S(1)}, bf16[2,96,768]{2,1,0:T(8,128)(2,1)S(1)}, u32[]{:S(2)}, u32[]{:S(2)}) %collective-permute-start.19) | collective-permute-done | bytes 294944 | tf_op jit(solution)/shard_map/ppermute | solution.py:371
  298.7 0.1 collective-permute-start.21
  298.8 3.2 collective-permute-start.20
  302.0 2.0 collective-permute-done.7
  304.3 3.2 collective-permute-start.8
  307.5 8.8 %collective-permute-done.21.minus = bf16[4,96,768]{2,1,0:T(8,128)(2,1)S(1)} collective-permute-done((bf16[4,96,768]{2,1,0:T(8,128)(2,1)S(1)}, bf16[4,96,768]{2,1,0:T(8,128)(2,1)S(1)}, u32[]{:S(2)}, u32[]{:S(2)}) %collective-permute-start.21) | collective-permute-done | bytes 589856 | tf_op jit(solution)/shard_map/ppermute | solution.py:367
  316.4 3.3 collective-permute-start.23
  319.7 9.2 %collective-permute-done.9.minus = bf16[4,48,1536]{2,1,0:T(8,128)(2,1)S(1)} collective-permute-done((bf16[4,48,1536]{2,1,0:T(8,128)(2,1)S(1)}, bf16[4,48,1536]{2,1,0:T(8,128)(2,1)S(1)}, u32[]{:S(2)}, u32[]{:S(2)}) %collective-permute-start.9) | collective-permute-done | bytes 589856 | tf_op jit(solution)/shard_map/ppermute | solution.py:367
  328.9 0.8 slice.148
  329.6 0.8 slice.149
  330.5 3.2 collective-permute-start.11
  333.7 1.6 collective-permute-done.22.cross_a
  335.3 72.7 %assemble.3 = bf16[1536,768]{1,0:T(8,128)(2,1)} custom-call(s32[1]{0:T(128)} %bitcast.rep_ref, bf16[4,96,768]{2,1,0:T(8,128)(2,1)} %copy-done.12, bf16[4,96,768]{2,1,0:T(8,128)(2,1)} %copy-done.15, bf16[4,96,768]{2,1,0:T(8,128)(2,1)} %copy-done.14, bf16[2,96,768]{2,1,0:T(8,128)(2,1)} %collective-permute-done.22.cross_a, ...), custom_call_target="tpu_custom_call" | custom-call | bytes 5000000 | tf_op jit(solution)/shard_map/assemble/pallas_call | solution.py:421
  408.1 72.7 %assemble.2 = bf16[768,1536]{1,0:T(8,128)(2,1)} custom-call(s32[1]{0:T(128)} %bitcast.rep_ref, bf16[4,48,1536]{2,1,0:T(8,128)(2,1)} %copy-done.13, bf16[4,48,1536]{2,1,0:T(8,128)(2,1)} %copy-done.17, bf16[4,48,1536]{2,1,0:T(8,128)(2,1)} %copy-done.16, bf16[2,48,1536]{2,1,0:T(8,128)(2,1)} %collective-permute-done.10.cross_a, ...), custom_call_target="tpu_custom_call" | custom-call | bytes 5000000 | tf_op jit(solution)/shard_map/assemble/pallas_call | solution.py:421
  (80 shorter events, 1.6 us)
Async XLA Ops:
  1.4 35.9 %copy-start.8 = (bf16[1,768,1536]{2,1,0:T(8,128)(2,1)S(1)}, bf16[1,768,1536]{2,1,0:T(8,128)(2,1)}, u32[]{:S(2)}) copy-start(bf16[1,768,1536]{2,1,0:T(8,128)(2,1)} %param.8) | copy-start | bytes 7077892
  44.0 1.1 copy-start.10
  45.2 30.4 %copy-start.23 = (f32[1,2,128,2]{2,3,1,0:T(2,128)S(1)}, f32[1,2,128,2]{2,3,1,0:T(2,128)}, u32[]{:S(2)}) copy-start(f32[1,2,128,2]{2,3,1,0:T(2,128)} %param.15) | copy-start | bytes 6148
  45.2 30.5 %copy-start.20 = (bf16[1,2,128,768]{3,2,1,0:T(8,128)(2,1)S(1)}, bf16[1,2,128,768]{3,2,1,0:T(8,128)(2,1)}, u32[]{:S(2)}) copy-start(bf16[1,2,128,768]{3,2,1,0:T(8,128)(2,1)} %param.13) | copy-start | bytes 1179652
  45.2 26.9 %all-to-all-start.2 = ((bf16[16,32,768]{2,1,0:T(8,128)(2,1)}), bf16[16,32,768]{2,1,0:T(8,128)(2,1)S(1)}, u32[]{:S(2)}, u32[]{:S(2)}) async-start(bf16[16,32,768]{2,1,0:T(8,128)(2,1)} %bitcast.14), calls=%async_computation.2 | async-start | bytes 1572864 | tf_op jit(solution)/shard_map/all_to_all | solution.py:443
  72.0 26.8 %all-to-all-start.1 = ((bf16[16,32,768]{2,1,0:T(8,128)(2,1)}), bf16[16,32,768]{2,1,0:T(8,128)(2,1)S(1)}, u32[]{:S(2)}, u32[]{:S(2)}) async-start(bf16[16,32,768]{2,1,0:T(8,128)(2,1)} %bitcast.9), calls=%async_computation.1 | async-start | bytes 1572864 | tf_op jit(solution)/shard_map/all_to_all | solution.py:443
  125.3 15.7 %copy-start = (bf16[16,32,768]{2,1,0:T(8,128)(2,1)}, bf16[16,32,768]{2,1,0:T(8,128)(2,1)S(1)}, u32[]{:S(2)}) copy-start(bf16[16,32,768]{2,1,0:T(8,128)(2,1)S(1)} %all_to_all.31) | copy-start | bytes 2359300
  141.1 0.9 copy-start.2
  142.0 1.2 copy-start.9
  143.1 55.8 %copy-start.1 = (bf16[16,32,768]{2,1,0:T(8,128)(2,1)S(1)}, bf16[16,32,768]{2,1,0:T(8,128)(2,1)}, u32[]{:S(2)}) copy-start(bf16[16,32,768]{2,1,0:T(8,128)(2,1)} %copy-done) | copy-start | bytes 2359300
  143.1 26.9 %all-to-all-start.4 = ((bf16[16,32,768]{2,1,0:T(8,128)(2,1)}), bf16[16,32,768]{2,1,0:T(8,128)(2,1)S(1)}, u32[]{:S(2)}, u32[]{:S(2)}) async-start(bf16[16,32,768]{2,1,0:T(8,128)(2,1)} %bitcast.92), calls=%async_computation.4 | async-start | bytes 1572864 | tf_op jit(solution)/shard_map/all_to_all | solution.py:443
  172.2 26.8 %all-to-all-start.5 = ((bf16[16,32,768]{2,1,0:T(8,128)(2,1)}), bf16[16,32,768]{2,1,0:T(8,128)(2,1)S(1)}, u32[]{:S(2)}, u32[]{:S(2)}) async-start(bf16[16,32,768]{2,1,0:T(8,128)(2,1)} %bitcast.22), calls=%async_computation.5 | async-start | bytes 1572864 | tf_op jit(solution)/shard_map/all_to_all | solution.py:443
  199.0 1.4 copy-start.11
  211.6 15.6 %copy-start.5 = (bf16[4,96,768]{2,1,0:T(8,128)(2,1)}, bf16[4,96,768]{2,1,0:T(8,128)(2,1)S(1)}, u32[]{:S(2)}) copy-start(bf16[4,96,768]{2,1,0:T(8,128)(2,1)S(1)} %get-tuple-element.35) | copy-start | bytes 1769476
  211.6 15.6 %copy-start.7 = (bf16[2,96,768]{2,1,0:T(8,128)(2,1)}, bf16[2,96,768]{2,1,0:T(8,128)(2,1)S(1)}, u32[]{:S(2)}) copy-start(bf16[2,96,768]{2,1,0:T(8,128)(2,1)S(1)} %get-tuple-element.37) | copy-start | bytes 884740
  211.6 18.5 %collective-permute-start.12 = (bf16[4,96,768]{2,1,0:T(8,128)(2,1)S(1)}, bf16[4,96,768]{2,1,0:T(8,128)(2,1)S(1)}, u32[]{:S(2)}, u32[]{:S(2)}) collective-permute-start(bf16[4,96,768]{2,1,0:T(8,128)(2,1)S(1)} %get-tuple-element.36), channel_id=1, source_target_pairs={{0,48},{16,0},{32,16},{48,32},{64,112},{80,64},{96,80},{112,96},{1... | collective-permute-start | bytes 1769480 | tf_op jit(solution)/shard_map/ppermute | solution.py:367
  227.2 0.8 copy-start.3
  228.0 26.1 %copy-start.4 = (bf16[4,48,1536]{2,1,0:T(8,128)(2,1)S(1)}, bf16[4,48,1536]{2,1,0:T(8,128)(2,1)}, u32[]{:S(2)}) copy-start(bf16[4,48,1536]{2,1,0:T(8,128)(2,1)} %copy-done.3) | copy-start | bytes 1769476
  228.0 13.0 %collective-permute-start = (bf16[4,48,1536]{2,1,0:T(8,128)(2,1)S(1)}, bf16[4,48,1536]{2,1,0:T(8,128)(2,1)S(1)}, u32[]{:S(2)}, u32[]{:S(2)}) collective-permute-start(bf16[4,48,1536]{2,1,0:T(8,128)(2,1)S(1)} %get-tuple-element.30), channel_id=1, source_target_pairs={{0,48},{16,0},{32,16},{48,32},{64,112},{80,64},{96,80},{112,96},{1... | collective-permute-start | bytes 1769480 | tf_op jit(solution)/shard_map/ppermute | solution.py:367
  228.8 17.0 %collective-permute-start.13 = (bf16[4,96,768]{2,1,0:T(8,128)(2,1)}, bf16[4,96,768]{2,1,0:T(8,128)(2,1)}, u32[]{:S(2)}, u32[]{:S(2)}) collective-permute-start(bf16[4,96,768]{2,1,0:T(8,128)(2,1)} %get-tuple-element.38), channel_id=1, source_target_pairs={{0,16},{16,32},{32,48},{48,0},{64,80},{80,96},{96,112},{112,64},{1... | collective-permute-start | bytes 1769480 | tf_op jit(solution)/shard_map/ppermute | solution.py:367
  230.1 24.1 %collective-permute-start.1 = (bf16[4,48,1536]{2,1,0:T(8,128)(2,1)}, bf16[4,48,1536]{2,1,0:T(8,128)(2,1)S(1)}, u32[]{:S(2)}, u32[]{:S(2)}) collective-permute-start(bf16[4,48,1536]{2,1,0:T(8,128)(2,1)} %get-tuple-element.32), channel_id=1, source_target_pairs={{0,16},{16,32},{32,48},{48,0},{64,80},{80,96},{96,112},{112,64},{1... | collective-permute-start | bytes 1769480 | tf_op jit(solution)/shard_map/ppermute | solution.py:367
  230.1 11.8 %copy-start.18 = (bf16[4,96,768]{2,1,0:T(8,128)(2,1)}, bf16[4,96,768]{2,1,0:T(8,128)(2,1)S(1)}, u32[]{:S(2)}) copy-start(bf16[4,96,768]{2,1,0:T(8,128)(2,1)S(1)} %collective-permute-done.12) | copy-start | bytes 1769476
  231.0 14.8 %collective-permute-start.15 = (bf16[2,96,768]{2,1,0:T(8,128)(2,1)}, bf16[2,96,768]{2,1,0:T(8,128)(2,1)}, u32[]{:S(2)}, u32[]{:S(2)}) collective-permute-start(bf16[2,96,768]{2,1,0:T(8,128)(2,1)} %add_convert_fusion.1), channel_id=1, source_target_pairs={{0,48},{16,0},{32,16},{48,32},{64,112},{80,64},{96,80},{112,96},{1... | collective-permute-start | bytes 884744 | tf_op jit(solution)/shard_map/ppermute | solution.py:367
  241.1 21.2 %copy-start.6 = (bf16[4,96,768]{2,1,0:T(8,128)(2,1)S(1)}, bf16[4,96,768]{2,1,0:T(8,128)(2,1)}, u32[]{:S(2)}) copy-start(bf16[4,96,768]{2,1,0:T(8,128)(2,1)} %copy-done.5) | copy-start | bytes 1769476
  241.9 12.3 %collective-permute-start.3 = (bf16[2,48,1536]{2,1,0:T(8,128)(2,1)}, bf16[2,48,1536]{2,1,0:T(8,128)(2,1)}, u32[]{:S(2)}, u32[]{:S(2)}) collective-permute-start(bf16[2,48,1536]{2,1,0:T(8,128)(2,1)} %add_convert_fusion.4), channel_id=1, source_target_pairs={{0,48},{16,0},{32,16},{48,32},{64,112},{80,64},{96,80},{112,96},{1... | collective-permute-start | bytes 884744 | tf_op jit(solution)/shard_map/ppermute | solution.py:367
  245.2 17.1 %copy-start.19 = (bf16[4,96,768]{2,1,0:T(8,128)(2,1)S(1)}, bf16[4,96,768]{2,1,0:T(8,128)(2,1)}, u32[]{:S(2)}) copy-start(bf16[4,96,768]{2,1,0:T(8,128)(2,1)} %copy-done.18) | copy-start | bytes 1769476
  247.3 15.0 %collective-permute-start.14 = (bf16[2,96,768]{2,1,0:T(8,128)(2,1)S(1)}, bf16[2,96,768]{2,1,0:T(8,128)(2,1)S(1)}, u32[]{:S(2)}, u32[]{:S(2)}) collective-permute-start(bf16[2,96,768]{2,1,0:T(8,128)(2,1)S(1)} %get-tuple-element.44), channel_id=1, source_target_pairs={{0,16},{16,32},{32,48},{48,0},{64,80},{80,96},{96,112},{112,64},{1... | collective-permute-start | bytes 884744 | tf_op jit(solution)/shard_map/ppermute | solution.py:367
  247.4 14.9 %collective-permute-start.16 = (bf16[2,96,768]{2,1,0:T(8,128)(2,1)S(1)}, bf16[2,96,768]{2,1,0:T(8,128)(2,1)S(1)}, u32[]{:S(2)}, u32[]{:S(2)}) collective-permute-start(bf16[2,96,768]{2,1,0:T(8,128)(2,1)S(1)} %get-tuple-element.45), channel_id=1, source_target_pairs={{0,64},{16,80},{32,96},{48,112},{64,0},{80,16},{96,32},{112,48},{1... | collective-permute-start | bytes 884744 | tf_op jit(solution)/shard_map/ppermute | solution.py:371
  255.3 18.1 %copy-start.21 = (f32[1,96,768]{2,1,0:T(8,128)S(1)}, f32[1,96,768]{2,1,0:T(8,128)}, u32[]{:S(2)}) copy-start(f32[1,96,768]{2,1,0:T(8,128)} %param.11) | copy-start | bytes 884740
  255.3 12.7 %collective-permute-start.2 = (bf16[2,48,1536]{2,1,0:T(8,128)(2,1)S(1)}, bf16[2,48,1536]{2,1,0:T(8,128)(2,1)S(1)}, u32[]{:S(2)}, u32[]{:S(2)}) collective-permute-start(bf16[2,48,1536]{2,1,0:T(8,128)(2,1)S(1)} %get-tuple-element.46), channel_id=1, source_target_pairs={{0,16},{16,32},{32,48},{48,0},{64,80},{80,96},{96,112},{112,64},{1... | collective-permute-start | bytes 884744 | tf_op jit(solution)/shard_map/ppermute | solution.py:367
  256.1 27.4 %copy-start.22 = (f32[1,48,1536]{2,1,0:T(8,128)S(1)}, f32[1,48,1536]{2,1,0:T(8,128)}, u32[]{:S(2)}) copy-start(f32[1,48,1536]{2,1,0:T(8,128)} %param.10) | copy-start | bytes 884740
  256.1 12.5 %collective-permute-start.4 = (bf16[2,48,1536]{2,1,0:T(8,128)(2,1)S(1)}, bf16[2,48,1536]{2,1,0:T(8,128)(2,1)S(1)}, u32[]{:S(2)}, u32[]{:S(2)}) collective-permute-start(bf16[2,48,1536]{2,1,0:T(8,128)(2,1)S(1)} %get-tuple-element.47), channel_id=1, source_target_pairs={{0,64},{16,80},{32,96},{48,112},{64,0},{80,16},{96,32},{112,48},{1... | collective-permute-start | bytes 884744 | tf_op jit(solution)/shard_map/ppermute | solution.py:371
  262.5 10.9 %collective-permute-start.17 = (bf16[96,768]{1,0:T(8,128)(2,1)S(1)}, bf16[96,768]{1,0:T(8,128)(2,1)S(1)}, u32[]{:S(2)}, u32[]{:S(2)}) collective-permute-start(bf16[96,768]{1,0:T(8,128)(2,1)S(1)} %fusion.9), channel_id=1, source_target_pairs={{0,128},{16,144},{32,160},{48,176},{64,192},{80,208},{96,224},{112... | collective-permute-start | bytes 442376 | tf_op jit(solution)/shard_map/ppermute | solution.py:371
  268.8 14.7 %collective-permute-start.5 = (bf16[48,1536]{1,0:T(8,128)(2,1)S(1)}, bf16[48,1536]{1,0:T(8,128)(2,1)S(1)}, u32[]{:S(2)}, u32[]{:S(2)}) collective-permute-start(bf16[48,1536]{1,0:T(8,128)(2,1)S(1)} %fusion.8), channel_id=1, source_target_pairs={{0,128},{16,144},{32,160},{48,176},{64,192},{80,208},{96,224},{112... | collective-permute-start | bytes 442376 | tf_op jit(solution)/shard_map/ppermute | solution.py:371
  275.1 10.8 %collective-permute-start.18 = (bf16[96,768]{1,0:T(8,128)(2,1)S(1)}, bf16[96,768]{1,0:T(8,128)(2,1)S(1)}, u32[]{:S(2)}, u32[]{:S(2)}) collective-permute-start(bf16[96,768]{1,0:T(8,128)(2,1)S(1)} %get-tuple-element.41), channel_id=1, source_target_pairs={{0,128},{16,144},{32,160},{48,176},{64,192},{80,208},{96,224},{112... | collective-permute-start | bytes 442376 | tf_op jit(solution)/shard_map/ppermute | solution.py:371
  285.2 7.9 %collective-permute-start.6 = (bf16[48,1536]{1,0:T(8,128)(2,1)S(1)}, bf16[48,1536]{1,0:T(8,128)(2,1)S(1)}, u32[]{:S(2)}, u32[]{:S(2)}) collective-permute-start(bf16[48,1536]{1,0:T(8,128)(2,1)S(1)} %get-tuple-element.43), channel_id=1, source_target_pairs={{0,128},{16,144},{32,160},{48,176},{64,192},{80,208},{96,224},{112... | collective-permute-start | bytes 442376 | tf_op jit(solution)/shard_map/ppermute | solution.py:371
  286.0 12.6 %collective-permute-start.19 = (bf16[2,96,768]{2,1,0:T(8,128)(2,1)S(1)}, bf16[2,96,768]{2,1,0:T(8,128)(2,1)S(1)}, u32[]{:S(2)}, u32[]{:S(2)}) collective-permute-start(bf16[2,96,768]{2,1,0:T(8,128)(2,1)S(1)} %pad_maximum_fusion.3), channel_id=1, source_target_pairs={{0,64},{16,80},{32,96},{48,112},{64,0},{80,16},{96,32},{112,48},{1... | collective-permute-start | bytes 884744 | tf_op jit(solution)/shard_map/ppermute | solution.py:371
  293.1 10.9 %collective-permute-start.7 = (bf16[2,48,1536]{2,1,0:T(8,128)(2,1)S(1)}, bf16[2,48,1536]{2,1,0:T(8,128)(2,1)S(1)}, u32[]{:S(2)}, u32[]{:S(2)}) collective-permute-start(bf16[2,48,1536]{2,1,0:T(8,128)(2,1)S(1)} %pad_maximum_fusion.2), channel_id=1, source_target_pairs={{0,64},{16,80},{32,96},{48,112},{64,0},{80,16},{96,32},{112,48},{1... | collective-permute-start | bytes 884744 | tf_op jit(solution)/shard_map/ppermute | solution.py:371
  298.7 36.6 %copy-start.12 = (bf16[4,96,768]{2,1,0:T(8,128)(2,1)}, bf16[4,96,768]{2,1,0:T(8,128)(2,1)S(1)}, u32[]{:S(2)}) copy-start(bf16[4,96,768]{2,1,0:T(8,128)(2,1)S(1)} %pad_maximum_fusion.1.home) | copy-start | bytes 1769476
  298.7 17.6 %collective-permute-start.21 = (bf16[4,96,768]{2,1,0:T(8,128)(2,1)S(1)}, bf16[4,96,768]{2,1,0:T(8,128)(2,1)S(1)}, u32[]{:S(2)}, u32[]{:S(2)}) collective-permute-start(bf16[4,96,768]{2,1,0:T(8,128)(2,1)S(1)} %pad_maximum_fusion.1.home), channel_id=1, source_target_pairs={{0,16},{16,32},{32,48},{48,0},{64,80},{80,96},{96,112},{112,64},{1... | collective-permute-start | bytes 1769480 | tf_op jit(solution)/shard_map/ppermute | solution.py:367
  298.8 17.5 %collective-permute-start.20 = (bf16[4,96,768]{2,1,0:T(8,128)(2,1)S(1)}, bf16[4,96,768]{2,1,0:T(8,128)(2,1)S(1)}, u32[]{:S(2)}, u32[]{:S(2)}) collective-permute-start(bf16[4,96,768]{2,1,0:T(8,128)(2,1)S(1)} %pad_maximum_fusion.1.home), channel_id=1, source_target_pairs={{0,48},{16,0},{32,16},{48,32},{64,112},{80,64},{96,80},{112,96},{1... | collective-permute-start | bytes 1769480 | tf_op jit(solution)/shard_map/ppermute | solution.py:367
  304.1 103.9 %copy-start.13 = (bf16[4,48,1536]{2,1,0:T(8,128)(2,1)}, bf16[4,48,1536]{2,1,0:T(8,128)(2,1)S(1)}, u32[]{:S(2)}) copy-start(bf16[4,48,1536]{2,1,0:T(8,128)(2,1)S(1)} %pad_maximum_fusion.home) | copy-start | bytes 1769476
  304.1 24.7 %collective-permute-start.9 = (bf16[4,48,1536]{2,1,0:T(8,128)(2,1)S(1)}, bf16[4,48,1536]{2,1,0:T(8,128)(2,1)S(1)}, u32[]{:S(2)}, u32[]{:S(2)}) collective-permute-start(bf16[4,48,1536]{2,1,0:T(8,128)(2,1)S(1)} %pad_maximum_fusion.home), channel_id=1, source_target_pairs={{0,16},{16,32},{32,48},{48,0},{64,80},{80,96},{96,112},{112,64},{1... | collective-permute-start | bytes 1769480 | tf_op jit(solution)/shard_map/ppermute | solution.py:367
  304.3 25.4 %collective-permute-start.8 = (bf16[4,48,1536]{2,1,0:T(8,128)(2,1)S(1)}, bf16[4,48,1536]{2,1,0:T(8,128)(2,1)S(1)}, u32[]{:S(2)}, u32[]{:S(2)}) collective-permute-start(bf16[4,48,1536]{2,1,0:T(8,128)(2,1)S(1)} %pad_maximum_fusion.home), channel_id=1, source_target_pairs={{0,48},{16,0},{32,16},{48,32},{64,112},{80,64},{96,80},{112,96},{1... | collective-permute-start | bytes 1769480 | tf_op jit(solution)/shard_map/ppermute | solution.py:367
  316.2 19.1 %copy-start.14 = (bf16[4,96,768]{2,1,0:T(8,128)(2,1)}, bf16[4,96,768]{2,1,0:T(8,128)(2,1)S(1)}, u32[]{:S(2)}) copy-start(bf16[4,96,768]{2,1,0:T(8,128)(2,1)S(1)} %collective-permute-done.21.minus) | copy-start | bytes 1769476
  316.3 19.0 %collective-permute-start.22 = (bf16[2,96,768]{2,1,0:T(8,128)(2,1)S(1)}, bf16[2,96,768]{2,1,0:T(8,128)(2,1)}, u32[]{:S(2)}, u32[]{:S(2)}) collective-permute-start(bf16[2,96,768]{2,1,0:T(8,128)(2,1)S(1)} %slice.158), channel_id=1, source_target_pairs={{0,16},{16,32},{32,48},{48,0},{64,80},{80,96},{96,112},{112,64},{1... | collective-permute-start | bytes 884744 | tf_op jit(solution)/shard_map/ppermute | solution.py:367
  316.4 18.9 %copy-start.15 = (bf16[4,96,768]{2,1,0:T(8,128)(2,1)}, bf16[4,96,768]{2,1,0:T(8,128)(2,1)S(1)}, u32[]{:S(2)}) copy-start(bf16[4,96,768]{2,1,0:T(8,128)(2,1)S(1)} %collective-permute-done.20.plus) | copy-start | bytes 1769476
  316.4 18.9 %collective-permute-start.23 = (bf16[2,96,768]{2,1,0:T(8,128)(2,1)S(1)}, bf16[2,96,768]{2,1,0:T(8,128)(2,1)}, u32[]{:S(2)}, u32[]{:S(2)}) collective-permute-start(bf16[2,96,768]{2,1,0:T(8,128)(2,1)S(1)} %slice.159), channel_id=1, source_target_pairs={{0,48},{16,0},{32,16},{48,32},{64,112},{80,64},{96,80},{112,96},{1... | collective-permute-start | bytes 884744 | tf_op jit(solution)/shard_map/ppermute | solution.py:367
  328.9 79.2 %copy-start.16 = (bf16[4,48,1536]{2,1,0:T(8,128)(2,1)}, bf16[4,48,1536]{2,1,0:T(8,128)(2,1)S(1)}, u32[]{:S(2)}) copy-start(bf16[4,48,1536]{2,1,0:T(8,128)(2,1)S(1)} %collective-permute-done.9.minus) | copy-start | bytes 1769476
  329.6 78.5 %collective-permute-start.10 = (bf16[2,48,1536]{2,1,0:T(8,128)(2,1)}, bf16[2,48,1536]{2,1,0:T(8,128)(2,1)}, u32[]{:S(2)}, u32[]{:S(2)}) collective-permute-start(bf16[2,48,1536]{2,1,0:T(8,128)(2,1)} %slice.148), channel_id=1, source_target_pairs={{0,16},{16,32},{32,48},{48,0},{64,80},{80,96},{96,112},{112,64},{1... | collective-permute-start | bytes 884744 | tf_op jit(solution)/shard_map/ppermute | solution.py:367
  329.6 78.4 %copy-start.17 = (bf16[4,48,1536]{2,1,0:T(8,128)(2,1)}, bf16[4,48,1536]{2,1,0:T(8,128)(2,1)S(1)}, u32[]{:S(2)}) copy-start(bf16[4,48,1536]{2,1,0:T(8,128)(2,1)S(1)} %collective-permute-done.8.plus) | copy-start | bytes 1769476
  330.5 77.6 %collective-permute-start.11 = (bf16[2,48,1536]{2,1,0:T(8,128)(2,1)}, bf16[2,48,1536]{2,1,0:T(8,128)(2,1)}, u32[]{:S(2)}, u32[]{:S(2)}) collective-permute-start(bf16[2,48,1536]{2,1,0:T(8,128)(2,1)} %slice.149), channel_id=1, source_target_pairs={{0,48},{16,0},{32,16},{48,32},{64,112},{80,64},{96,80},{112,96},{1... | collective-permute-start | bytes 884744 | tf_op jit(solution)/shard_map/ppermute | solution.py:367

commit v2 on v1

--- a/solution.py
+++ b/solution.py
@@ -53,17 +53,21 @@
     return x * half, slope
 
 
+RATE, DECAY = 0.004, 0.1
+KEEP = 1.0 - RATE * DECAY
+
+
 def after_one(weight, grad):
-    ratio = grad / (jnp.abs(grad) + 0.01)
-    return weight - 0.004 * (ratio + 0.1 * weight)
+    return KEEP * weight - RATE * (grad * pl.reciprocal(jnp.abs(grad) + 0.01))
 
 
 def change_of_two(weight, grad_one, grad_two):
-    theta = after_one(weight, grad_one)
     first = (0.09 / 0.19) * grad_one + (0.1 / 0.19) * grad_two
     second = (0.0475 / 0.0975) * (grad_one * grad_one) + (0.05 / 0.0975) * (grad_two * grad_two)
-    ratio = first / (jnp.sqrt(second) + 0.01)
-    return weight - (theta - 0.004 * (ratio + 0.1 * theta))
+    below_two = second * lax.rsqrt(second + 1e-30) + 0.01
+    below_one = jnp.abs(grad_one) + 0.01
+    over = KEEP * (grad_one * below_two) + first * below_one
+    return (1.0 - KEEP * KEEP) * weight + RATE * (over * pl.reciprocal(below_one * below_two))
 
 
 def params(limit=48):
@@ -157,7 +161,7 @@
         ],
         scratch_shapes=[pltpu.VMEM((slots, width), F32)],
         compiler_params=params(),
-        cost_estimate=cost(2.4e9, 1e7),
+        cost_estimate=cost(7e9, 1e7),
         name="forward",
     )(rows, w_in, w_out)
 
@@ -241,7 +245,7 @@
         ],
         scratch_shapes=[pltpu.VMEM((slots, width), F32), pltpu.VMEM((width, slots), BF16)],
         compiler_params=params(),
-        cost_estimate=cost(7e9, 2e7),
+        cost_estimate=cost(1.5e10, 2e7),
         name="turn",
     )(rows, next_rows, cot, w_in, w_out, hidden, active)
 
@@ -256,16 +260,11 @@
 HALVES = ((1, 3), (0, 2))
 
 
-def store_change(rep, band, w_ref, grad_one, grad_two, outs):
-    x, z = rep % NX, rep // NX
-    for k in range(NX):
-        for half, members in enumerate(HALVES):
-            name, at = PARTS[k][half]
-            for i, m in enumerate(members):
-                first = pl.multiple_of((jnp.bitwise_xor(z, m) * NX + (x + k) % NX) * band, 16)
-                rows = pl.ds(first, band)
-                change = change_of_two(w_ref[rows, :].astype(F32), grad_one[rows, :], grad_two[rows, :])
-                outs[name][at + i] = change.astype(BF16)
+def store_band(k, m, rows, w_ref, grad_one, grad_two, outs):
+    half = 0 if m in HALVES[0] else 1
+    name, at = PARTS[k][half]
+    change = change_of_two(w_ref[rows, :].astype(F32), grad_one[rows, :], grad_two[rows, :])
+    outs[name][at + HALVES[half].index(m)] = change.astype(BF16)
 
 
 def change_out_kernel(rep_ref, w_ref, act_one, cot_one, act_two, cot_two, *rest):
@@ -274,31 +273,47 @@
     grad_one[...] = dot(act_one[...], cot_one[...], 0, 0)
     grad_two[...] = dot(act_two[...], cot_two[...], 0, 0)
     band = outs["own"].shape[1]
-    store_change(rep_ref[0], band, w_ref, grad_one, grad_two, outs)
-
-
-def change_out(rep, replicas, w_out, act_one, cot_one, act_two, cot_two, tile=256):
+    x = rep_ref[0] % NX
+    for m in range(NZ):
+
+        @pl.when(pl.program_id(0) == m)
+        def _():
+            for k in range(NX):
+                rows = pl.ds(pl.multiple_of((x + k) % NX * band, 16), band)
+                store_band(k, m, rows, w_ref, grad_one, grad_two, outs)
+
+
+def change_out(rep, replicas, w_out, act_one, cot_one, act_two, cot_two):
     slots, hid = act_one.shape
     width = cot_one.shape[1]
     band = hid // replicas
-    act = pl.BlockSpec((slots, hid), lambda i: (0, 0))
-    cot = pl.BlockSpec((slots, tile), lambda i: (0, i))
+    tile = band * NX
+
+    def z_of(i, rep_ref):
+        return jnp.bitwise_xor(rep_ref[0] // NX, i)
+
+    act = pl.BlockSpec((slots, tile), lambda i, r: (0, z_of(i, r)))
+    cot = pl.BlockSpec((slots, width), lambda i, r: (0, 0))
     return pl.pallas_call(
         change_out_kernel,
-        grid=(width // tile,),
-        in_specs=[
-            pl.BlockSpec(memory_space=pltpu.SMEM),
-            pl.BlockSpec((hid, tile), lambda i: (0, i)),
-            act,
-            cot,
-            act,
-            cot,
-        ],
-        out_specs=[pl.BlockSpec((n, band, tile), lambda i: (0, 0, i)) for n in PART_SHARDS.values()],
+        grid_spec=pltpu.PrefetchScalarGridSpec(
+            num_scalar_prefetch=1,
+            grid=(NZ,),
+            in_specs=[
+                pl.BlockSpec((tile, width), lambda i, r: (z_of(i, r), 0)),
+                act,
+                cot,
+                act,
+                cot,
+            ],
+            out_specs=[
+                pl.BlockSpec((n, band, width), lambda i, r: (0, 0, 0)) for n in PART_SHARDS.values()
+            ],
+            scratch_shapes=[pltpu.VMEM((tile, width), F32), pltpu.VMEM((tile, width), F32)],
+        ),
         out_shape=[jax.ShapeDtypeStruct((n, band, width), BF16) for n in PART_SHARDS.values()],
-        scratch_shapes=[pltpu.VMEM((hid, tile), F32), pltpu.VMEM((hid, tile), F32)],
-        compiler_params=params(),
-        cost_estimate=cost(2.4e9, 1e7),
+        compiler_params=params(),
+        cost_estimate=cost(8e9, 1e7),
         name="change_out",
     )(rep, w_out, act_one, cot_one, act_two, cot_two)
 
@@ -319,7 +334,11 @@
     grad_one[...] = dot(turned_one[...], dh_one[...])
     grad_two[...] = dot(turned_two[...], dh_two)
     band = outs["own"].shape[1]
-    store_change(rep_ref[0], band, w_ref, grad_one, grad_two, outs)
+    x, z = rep_ref[0] % NX, rep_ref[0] // NX
+    for k in range(NX):
+        for m in range(NZ):
+            first = pl.multiple_of((jnp.bitwise_xor(z, m) * NX + (x + k) % NX) * band, 16)
+            store_band(k, m, pl.ds(first, band), w_ref, grad_one, grad_two, outs)
 
 
 def change_in(rep, replicas, w_in, rows_one, dh_one, rows_two, cot_two, theta_out, hidden_two, tile=256):
@@ -350,7 +369,7 @@
             pltpu.VMEM((width, slots), BF16),
         ],
         compiler_params=params(),
-        cost_estimate=cost(3.6e9, 1.5e7),
+        cost_estimate=cost(1.2e10, 1.5e7),
         name="change_in",
     )(rep, w_in, rows_one, dh_one, rows_two, cot_two, theta_out, hidden_two)
 
@@ -389,23 +408,17 @@
     return mine[0] + across.astype(F32)
 
 
-def assemble_kernel(rep_ref, home, plus, minus, cross_a, cross_b, out, sem):
+def assemble_kernel(rep_ref, home, plus, minus, cross_a, cross_b, out):
     x, z = rep_ref[0] % NX, rep_ref[0] // NX
     band = home.shape[1]
-    copies = []
-    for k, source in ((0, home), (1, plus), (3, minus), (2, None)):
+    for k in range(NX):
         for m in range(NZ):
-            if source is None:
-                half = cross_a if m < 2 else cross_b
-                block = half.at[m % 2]
+            if k == 2:
+                block = (cross_a if m < 2 else cross_b)[m % 2]
             else:
-                block = source.at[m]
+                block = (home, plus, None, minus)[k][m]
             first = pl.multiple_of((jnp.bitwise_xor(z, m) * NX + (x + k) % NX) * band, 16)
-            copies.append(pltpu.make_async_copy(block, out.at[pl.ds(first, band), :], sem.at[len(copies)]))
-    for copy in copies:
-        copy.start()
-    for copy in copies:
-        copy.wait()
+            out[pl.ds(first, band), :] = block
 
 
 def gather_from_owner(rep, own):
@@ -417,13 +430,19 @@
     plus = shift_x(home, -1)
     cross_a = shift_x(minus[:2], 1)
     cross_b = shift_x(plus[2:], -1)
-    any_spec = pl.BlockSpec(memory_space=pl.ANY)
+    tile = 384
+
+    def part(shards):
+        return pl.BlockSpec((shards, band, tile), lambda i: (0, 0, i))
+
+    rows = NZ * NX * band
     return pl.pallas_call(
         assemble_kernel,
-        in_specs=[pl.BlockSpec(memory_space=pltpu.SMEM)] + [any_spec] * 5,
-        out_specs=any_spec,
-        out_shape=jax.ShapeDtypeStruct((NZ * NX * band, columns), BF16),
-        scratch_shapes=[pltpu.SemaphoreType.DMA((NZ * NX,))],
+        grid=(columns // tile,),
+        in_specs=[pl.BlockSpec(memory_space=pltpu.SMEM)] + [part(n) for n in (4, 4, 4, 2, 2)],
+        out_specs=pl.BlockSpec((rows, tile), lambda i: (0, i)),
+        out_shape=jax.ShapeDtypeStruct((rows, columns), BF16),
+        compiler_params=params(),
         cost_estimate=cost(0, 5e6),
         name="assemble",
     )(rep, home, plus, minus, cross_a, cross_b)

time: 485 us -> 342 us (0.71)
  Pallas kernels: 198 us -> 54 us
    pallas_call x3, Pallas kernels: 157 us -> 13.5 us  [the longest x1 9.46 us: change_out(): pl.pallas_call(change_out_kernel, grid_spec=pltpu.PrefetchScalarGridSpec(...]
  transfers between devices with their start and end apart: 28 -> 28, of which waited for: 16 -> 17; matrix products, arithmetic and copies ran while one was open for 2% -> 3% of each run, Pallas kernels for 18% -> 5%
where the time goes in v2:
time: 342 us; the launch traced here: 338 us
  waiting for transfers between devices  141 us (41%)
  starting transfers between devices  65.6 us (19%)
  blocking collectives  60.4 us (18%)
  Pallas kernels  54 us (16%)
  other arithmetic  8.23 us (2%)
  local copies, waits for them, and re-layouts  8.01 us (2%)
    all_to_all x4, waiting for transfers between devices, exchange(): lax.all_to_all(block, 'exp', split_axis=0, concat_axis=0, tiled=True)  89.4 us
    all_to_all x2, blocking collectives, exchange(): lax.all_to_all(block, 'exp', split_axis=0, concat_axis=0, tiled=True)  60.4 us
    ppermute x16, waiting for transfers between devices, shift_x(): return lax.ppermute(array, 'rep', rep_permutation(step, 0))  29.9 us
    ppermute x16, starting transfers between devices, shift_x(): return lax.ppermute(array, 'rep', rep_permutation(step, 0))  26.1 us
    ppermute x8, starting transfers between devices, swap_z(): return lax.ppermute(array, 'rep', rep_permutation(0, flip))  25 us
    ppermute x8, waiting for transfers between devices, swap_z(): return lax.ppermute(array, 'rep', rep_permutation(0, flip))  22 us
    pallas_call x1, Pallas kernels, turn(): pl.pallas_call(turn_kernel, grid=(hid // tile,), in_specs=[whole, whole,...  15.2 us
    all_to_all x4, starting transfers between devices, exchange(): lax.all_to_all(block, 'exp', split_axis=0, concat_axis=0, tiled=True)  14.5 us
  transfers between devices with their start and end apart: 28, of which 17 were waited for; matrix products, arithmetic and copies ran while one was open for 3% of the time, Pallas kernels for 5%

profile of v2, /device:TPU:8, one launch (start us, length us, event | category | flops | bytes accessed | tf_op | source)
XLA Modules:
  0.0 338.4 jit_solution(6374316596000179961)
XLA Ops:
  0.6 0.7 fusion.13
  1.4 1.2 slice_bitcast_fusion.4
  2.7 0.8 place_frames.2
  3.5 33.9 %all_to_all.30 = bf16[16,32,768]{2,1,0:T(8,128)(2,1)S(1)} all-to-all(bf16[16,32,768]{2,1,0:T(8,128)(2,1)S(1)} %bitcast.79), channel_id=1, replica_groups=mesh['rep'=16,'exp'=16] {'exp'}, dimensions={0} | all-to-all | bytes 1572864 | tf_op jit(solution)/shard_map/all_to_all | solution.py:462
  37.4 6.6 %forward.1 = (f32[512,1536]{1,0:T(8,128)}, bf16[512,1536]{1,0:T(8,128)(2,1)S(1)}, bf16[512,768]{1,0:T(8,128)(2,1)}) custom-call(bf16[512,768]{1,0:T(8,128)(2,1)S(1)} %bitcast.83, bf16[768,1536]{1,0:T(8,128)(2,1)S(1)} %bitcast.101, bf16[1536,768]{1,0:T(8,128)(2,1)} %bitcast.112), custom_call_target="tpu_custom_call" | custom-call | flops 7000000000 | bytes 10000000 | tf_op jit(solution)/shard_map/forward/pallas_call | solution.py:148
  44.0 1.1 copy-done.9
  45.1 3.6 %all-to-all-start.2 = ((bf16[16,32,768]{2,1,0:T(8,128)(2,1)}), bf16[16,32,768]{2,1,0:T(8,128)(2,1)S(1)}, u32[]{:S(2)}, u32[]{:S(2)}) async-start(bf16[16,32,768]{2,1,0:T(8,128)(2,1)} %bitcast.14), calls=%async_computation.2 | async-start | bytes 1572864 | tf_op jit(solution)/shard_map/all_to_all | solution.py:462
  48.9 1.7 place_frames.3
  50.6 21.4 %all-to-all-done.2 = bf16[16,32,768]{2,1,0:T(8,128)(2,1)S(1)} async-done(((bf16[16,32,768]{2,1,0:T(8,128)(2,1)}), bf16[16,32,768]{2,1,0:T(8,128)(2,1)S(1)}, u32[]{:S(2)}, u32[]{:S(2)}) %all-to-all-start.2) | async-done | bytes 786464 | tf_op jit(solution)/shard_map/all_to_all | solution.py:462
  72.0 3.5 %all-to-all-start.1 = ((bf16[16,32,768]{2,1,0:T(8,128)(2,1)}), bf16[16,32,768]{2,1,0:T(8,128)(2,1)S(1)}, u32[]{:S(2)}, u32[]{:S(2)}) async-start(bf16[16,32,768]{2,1,0:T(8,128)(2,1)} %bitcast.9), calls=%async_computation.1 | async-start | bytes 1572864 | tf_op jit(solution)/shard_map/all_to_all | solution.py:462
  75.7 1.3 place_residue.2
  77.0 21.8 %all-to-all-done.1 = bf16[16,32,768]{2,1,0:T(8,128)(2,1)S(1)} async-done(((bf16[16,32,768]{2,1,0:T(8,128)(2,1)}), bf16[16,32,768]{2,1,0:T(8,128)(2,1)S(1)}, u32[]{:S(2)}, u32[]{:S(2)}) %all-to-all-start.1) | async-done | bytes 786464 | tf_op jit(solution)/shard_map/all_to_all | solution.py:462
  98.7 26.5 %all_to_all.31 = bf16[16,32,768]{2,1,0:T(8,128)(2,1)S(1)} all-to-all(bf16[16,32,768]{2,1,0:T(8,128)(2,1)S(1)} %bitcast.82), channel_id=1, replica_groups=mesh['rep'=16,'exp'=16] {'exp'}, dimensions={0} | all-to-all | bytes 1572864 | tf_op jit(solution)/shard_map/all_to_all | solution.py:462
  125.3 15.2 %turn.1 = (bf16[512,1536]{1,0:T(8,128)(2,1)S(1)}, bf16[1536,768]{1,0:T(8,128)(2,1)}, f32[512,1536]{1,0:T(8,128)}, bf16[512,1536]{1,0:T(8,128)(2,1)}, bf16[512,768]{1,0:T(8,128)(2,1)S(1)}) custom-call(bf16[512,768]{1,0:T(8,128)(2,1)S(1)} %bitcast.84, bf16[512,768]{1,0:T(8,128)(2,1)S(1)} %bitcast.86, bf16[512,768]{1,0:T(8,128)(2,1)S(1)} %bitcast.88, ...), custom_call_target="tpu_custom_call" | custom-call | flops 15000000512 | bytes 20000000 | tf_op jit(solution)/shard_map/turn/pallas_call | solution.py:226
  140.5 0.9 copy-done.2
  141.4 1.2 copy-done.11
  142.6 3.6 %all-to-all-start.4 = ((bf16[16,32,768]{2,1,0:T(8,128)(2,1)}), bf16[16,32,768]{2,1,0:T(8,128)(2,1)S(1)}, u32[]{:S(2)}, u32[]{:S(2)}) async-start(bf16[16,32,768]{2,1,0:T(8,128)(2,1)} %bitcast.92), calls=%async_computation.4 | async-start | bytes 1572864 | tf_op jit(solution)/shard_map/all_to_all | solution.py:462
  146.3 23.1 %all-to-all-done.4 = bf16[16,32,768]{2,1,0:T(8,128)(2,1)S(1)} async-done(((bf16[16,32,768]{2,1,0:T(8,128)(2,1)}), bf16[16,32,768]{2,1,0:T(8,128)(2,1)S(1)}, u32[]{:S(2)}, u32[]{:S(2)}) %all-to-all-start.4) | async-done | bytes 786464 | tf_op jit(solution)/shard_map/all_to_all | solution.py:462
  169.5 2.2 place_residue.3
  171.6 3.7 %all-to-all-start.5 = ((bf16[16,32,768]{2,1,0:T(8,128)(2,1)}), bf16[16,32,768]{2,1,0:T(8,128)(2,1)S(1)}, u32[]{:S(2)}, u32[]{:S(2)}) async-start(bf16[16,32,768]{2,1,0:T(8,128)(2,1)} %bitcast.22), calls=%async_computation.5 | async-start | bytes 1572864 | tf_op jit(solution)/shard_map/all_to_all | solution.py:462
  175.3 23.1 %all-to-all-done.5 = bf16[16,32,768]{2,1,0:T(8,128)(2,1)S(1)} async-done(((bf16[16,32,768]{2,1,0:T(8,128)(2,1)}), bf16[16,32,768]{2,1,0:T(8,128)(2,1)S(1)}, u32[]{:S(2)}, u32[]{:S(2)}) %all-to-all-start.5) | async-done | bytes 786464 | tf_op jit(solution)/shard_map/all_to_all | solution.py:462
  198.4 1.4 copy-done.10
  199.8 9.5 %change_out.1 = (bf16[4,96,768]{2,1,0:T(8,128)(2,1)S(1)}, bf16[4,96,768]{2,1,0:T(8,128)(2,1)}, bf16[2,96,768]{2,1,0:T(8,128)(2,1)S(1)}, bf16[2,96,768]{2,1,0:T(8,128)(2,1)S(1)}, bf16[4,96,768]{2,1,0:T(8,128)(2,1)S(1)}) custom-call(s32[1]{0:T(128)} %bitcast.rep_ref, bf16[1536,768]{1,0:T(8,128)(2,1)} %bitcast.114, bf16[512,1536]{1,0:T(8,128)(2,1)S(1)} %copy-done.10, ...), custom_call_target="tpu_custom_call" | custom-call | flops 8000000000 | bytes 10000000 | tf_op jit(solution)/shard_map/change_out/pallas_call | solution.py:297
  209.3 2.8 collective-permute-start.12
  212.0 12.6 %change_in.1 = (bf16[4,48,1536]{2,1,0:T(8,128)(2,1)S(1)}, bf16[4,48,1536]{2,1,0:T(8,128)(2,1)}, bf16[2,48,1536]{2,1,0:T(8,128)(2,1)S(1)}, bf16[2,48,1536]{2,1,0:T(8,128)(2,1)S(1)}, bf16[4,48,1536]{2,1,0:T(8,128)(2,1)S(1)}) custom-call(s32[1]{0:T(128)} %bitcast.rep_ref, bf16[768,1536]{1,0:T(8,128)(2,1)} %bitcast.100, bf16[512,768]{1,0:T(8,128)(2,1)S(1)} %bitcast.85, ...), custom_call_target="tpu_custom_call" | custom-call | flops 12000000000 | bytes 15000000 | tf_op jit(solution)/shard_map/change_in/pallas_call | solution.py:350
  224.7 0.8 copy-done.3
  225.5 0.8 collective-permute-start
  226.3 1.2 collective-permute-start.13
  227.5 0.9 add_convert_fusion.1
  228.4 3.2 collective-permute-start.15
  231.6 6.9 %collective-permute-done = bf16[4,48,1536]{2,1,0:T(8,128)(2,1)S(1)} collective-permute-done((bf16[4,48,1536]{2,1,0:T(8,128)(2,1)S(1)}, bf16[4,48,1536]{2,1,0:T(8,128)(2,1)S(1)}, u32[]{:S(2)}, u32[]{:S(2)}) %collective-permute-start) | collective-permute-done | bytes 589856 | tf_op jit(solution)/shard_map/ppermute | solution.py:386
  238.5 0.8 add_convert_fusion.4
  239.3 3.6 %collective-permute-start.3 = (bf16[2,48,1536]{2,1,0:T(8,128)(2,1)}, bf16[2,48,1536]{2,1,0:T(8,128)(2,1)}, u32[]{:S(2)}, u32[]{:S(2)}) collective-permute-start(bf16[2,48,1536]{2,1,0:T(8,128)(2,1)} %add_convert_fusion.4), channel_id=1, source_target_pairs={{0,48},{16,0},{32,16},{48,32},{64,112},{80,64},{96,80},{112,96},{1... | collective-permute-start | bytes 884744 | tf_op jit(solution)/shard_map/ppermute | solution.py:386
  242.9 0.2 collective-permute-done.13
  243.1 1.5 add_convert_fusion.2
  244.6 0.4 collective-permute-start.14
  245.0 6.8 %collective-permute-start.16 = (bf16[2,96,768]{2,1,0:T(8,128)(2,1)S(1)}, bf16[2,96,768]{2,1,0:T(8,128)(2,1)S(1)}, u32[]{:S(2)}, u32[]{:S(2)}) collective-permute-start(bf16[2,96,768]{2,1,0:T(8,128)(2,1)S(1)} %get-tuple-element.45), channel_id=1, source_target_pairs={{0,64},{16,80},{32,96},{48,112},{64,0},{80,16},{96,32},{112,48},{1... | collective-permute-start | bytes 884744 | tf_op jit(solution)/shard_map/ppermute | solution.py:390
  251.8 1.1 add_convert_fusion.5
  253.0 0.7 collective-permute-start.2
  253.7 6.0 %collective-permute-start.4 = (bf16[2,48,1536]{2,1,0:T(8,128)(2,1)S(1)}, bf16[2,48,1536]{2,1,0:T(8,128)(2,1)S(1)}, u32[]{:S(2)}, u32[]{:S(2)}) collective-permute-start(bf16[2,48,1536]{2,1,0:T(8,128)(2,1)S(1)} %get-tuple-element.47), channel_id=1, source_target_pairs={{0,64},{16,80},{32,96},{48,112},{64,0},{80,16},{96,32},{112,48},{1... | collective-permute-start | bytes 884744 | tf_op jit(solution)/shard_map/ppermute | solution.py:390
  259.8 0.1 convert_add_fusion
  259.9 5.5 %collective-permute-start.17 = (bf16[96,768]{1,0:T(8,128)(2,1)S(1)}, bf16[96,768]{1,0:T(8,128)(2,1)S(1)}, u32[]{:S(2)}, u32[]{:S(2)}) collective-permute-start(bf16[96,768]{1,0:T(8,128)(2,1)S(1)} %fusion.9), channel_id=1, source_target_pairs={{0,128},{16,144},{32,160},{48,176},{64,192},{80,208},{96,224},{112... | collective-permute-start | bytes 442376 | tf_op jit(solution)/shard_map/ppermute | solution.py:390
  265.4 0.6 collective-permute-done.4
  266.2 4.0 %collective-permute-start.5 = (bf16[48,1536]{1,0:T(8,128)(2,1)S(1)}, bf16[48,1536]{1,0:T(8,128)(2,1)S(1)}, u32[]{:S(2)}, u32[]{:S(2)}) collective-permute-start(bf16[48,1536]{1,0:T(8,128)(2,1)S(1)} %fusion.8), channel_id=1, source_target_pairs={{0,128},{16,144},{32,160},{48,176},{64,192},{80,208},{96,224},{112... | collective-permute-start | bytes 442376 | tf_op jit(solution)/shard_map/ppermute | solution.py:390
  270.2 0.6 collective-permute-done.17
  270.8 1.7 fusion.7
  272.6 0.8 collective-permute-start.18
  273.3 7.6 %collective-permute-done.5 = bf16[48,1536]{1,0:T(8,128)(2,1)S(1)} collective-permute-done((bf16[48,1536]{1,0:T(8,128)(2,1)S(1)}, bf16[48,1536]{1,0:T(8,128)(2,1)S(1)}, u32[]{:S(2)}, u32[]{:S(2)}) %collective-permute-start.5) | collective-permute-done | bytes 147488 | tf_op jit(solution)/shard_map/ppermute | solution.py:390
  280.9 1.7 fusion.6
  282.6 0.8 collective-permute-done.18
  283.4 1.8 collective-permute-start.19
  285.2 5.3 %collective-permute-done.6 = bf16[48,1536]{1,0:T(8,128)(2,1)S(1)} collective-permute-done((bf16[48,1536]{1,0:T(8,128)(2,1)S(1)}, bf16[48,1536]{1,0:T(8,128)(2,1)S(1)}, u32[]{:S(2)}, u32[]{:S(2)}) %collective-permute-start.6) | collective-permute-done | bytes 147488 | tf_op jit(solution)/shard_map/ppermute | solution.py:390
  290.7 5.2 %collective-permute-done.19 = bf16[2,96,768]{2,1,0:T(8,128)(2,1)S(1)} collective-permute-done((bf16[2,96,768]{2,1,0:T(8,128)(2,1)S(1)}, bf16[2,96,768]{2,1,0:T(8,128)(2,1)S(1)}, u32[]{:S(2)}, u32[]{:S(2)}) %collective-permute-start.19) | collective-permute-done | bytes 294944 | tf_op jit(solution)/shard_map/ppermute | solution.py:390
  296.0 3.2 collective-permute-start.20
  299.2 2.0 collective-permute-done.7
  301.5 3.2 collective-permute-start.8
  304.7 8.8 %collective-permute-done.21.minus = bf16[4,96,768]{2,1,0:T(8,128)(2,1)S(1)} collective-permute-done((bf16[4,96,768]{2,1,0:T(8,128)(2,1)S(1)}, bf16[4,96,768]{2,1,0:T(8,128)(2,1)S(1)}, u32[]{:S(2)}, u32[]{:S(2)}) %collective-permute-start.21) | collective-permute-done | bytes 589856 | tf_op jit(solution)/shard_map/ppermute | solution.py:386
  313.6 3.3 collective-permute-start.23
  316.9 9.2 %collective-permute-done.9.minus = bf16[4,48,1536]{2,1,0:T(8,128)(2,1)S(1)} collective-permute-done((bf16[4,48,1536]{2,1,0:T(8,128)(2,1)S(1)}, bf16[4,48,1536]{2,1,0:T(8,128)(2,1)S(1)}, u32[]{:S(2)}, u32[]{:S(2)}) %collective-permute-start.9) | collective-permute-done | bytes 589856 | tf_op jit(solution)/shard_map/ppermute | solution.py:386
  326.3 3.3 collective-permute-start.11
  329.6 2.9 collective-permute-done.22.cross_a
  332.4 1.8 assemble.3
  334.3 1.8 collective-permute-done.10.cross_a
  336.1 2.3 assemble.2
  (68 shorter events, 1.6 us)
Async XLA Ops:
  1.4 35.9 %copy-start.8 = (bf16[1,768,1536]{2,1,0:T(8,128)(2,1)S(1)}, bf16[1,768,1536]{2,1,0:T(8,128)(2,1)}, u32[]{:S(2)}) copy-start(bf16[1,768,1536]{2,1,0:T(8,128)(2,1)} %param.8) | copy-start | bytes 7077892
  44.0 1.1 copy-start.9
  45.1 30.4 %copy-start.17 = (f32[1,2,128,2]{2,3,1,0:T(2,128)S(1)}, f32[1,2,128,2]{2,3,1,0:T(2,128)}, u32[]{:S(2)}) copy-start(f32[1,2,128,2]{2,3,1,0:T(2,128)} %param.15) | copy-start | bytes 6148
  45.1 30.5 %copy-start.14 = (bf16[1,2,128,768]{3,2,1,0:T(8,128)(2,1)S(1)}, bf16[1,2,128,768]{3,2,1,0:T(8,128)(2,1)}, u32[]{:S(2)}) copy-start(bf16[1,2,128,768]{3,2,1,0:T(8,128)(2,1)} %param.13) | copy-start | bytes 1179652
  45.1 26.9 %all-to-all-start.2 = ((bf16[16,32,768]{2,1,0:T(8,128)(2,1)}), bf16[16,32,768]{2,1,0:T(8,128)(2,1)S(1)}, u32[]{:S(2)}, u32[]{:S(2)}) async-start(bf16[16,32,768]{2,1,0:T(8,128)(2,1)} %bitcast.14), calls=%async_computation.2 | async-start | bytes 1572864 | tf_op jit(solution)/shard_map/all_to_all | solution.py:462
  72.0 26.8 %all-to-all-start.1 = ((bf16[16,32,768]{2,1,0:T(8,128)(2,1)}), bf16[16,32,768]{2,1,0:T(8,128)(2,1)S(1)}, u32[]{:S(2)}, u32[]{:S(2)}) async-start(bf16[16,32,768]{2,1,0:T(8,128)(2,1)} %bitcast.9), calls=%async_computation.1 | async-start | bytes 1572864 | tf_op jit(solution)/shard_map/all_to_all | solution.py:462
  125.3 15.2 %copy-start = (bf16[16,32,768]{2,1,0:T(8,128)(2,1)}, bf16[16,32,768]{2,1,0:T(8,128)(2,1)S(1)}, u32[]{:S(2)}) copy-start(bf16[16,32,768]{2,1,0:T(8,128)(2,1)S(1)} %all_to_all.31) | copy-start | bytes 2359300
  140.5 0.9 copy-start.2
  141.4 1.2 copy-start.11
  142.6 55.8 %copy-start.1 = (bf16[16,32,768]{2,1,0:T(8,128)(2,1)S(1)}, bf16[16,32,768]{2,1,0:T(8,128)(2,1)}, u32[]{:S(2)}) copy-start(bf16[16,32,768]{2,1,0:T(8,128)(2,1)} %copy-done) | copy-start | bytes 2359300
  142.6 26.9 %all-to-all-start.4 = ((bf16[16,32,768]{2,1,0:T(8,128)(2,1)}), bf16[16,32,768]{2,1,0:T(8,128)(2,1)S(1)}, u32[]{:S(2)}, u32[]{:S(2)}) async-start(bf16[16,32,768]{2,1,0:T(8,128)(2,1)} %bitcast.92), calls=%async_computation.4 | async-start | bytes 1572864 | tf_op jit(solution)/shard_map/all_to_all | solution.py:462
  171.6 26.8 %all-to-all-start.5 = ((bf16[16,32,768]{2,1,0:T(8,128)(2,1)}), bf16[16,32,768]{2,1,0:T(8,128)(2,1)S(1)}, u32[]{:S(2)}, u32[]{:S(2)}) async-start(bf16[16,32,768]{2,1,0:T(8,128)(2,1)} %bitcast.22), calls=%async_computation.5 | async-start | bytes 1572864 | tf_op jit(solution)/shard_map/all_to_all | solution.py:462
  198.4 1.4 copy-start.10
  209.3 15.4 %copy-start.5 = (bf16[4,96,768]{2,1,0:T(8,128)(2,1)}, bf16[4,96,768]{2,1,0:T(8,128)(2,1)S(1)}, u32[]{:S(2)}) copy-start(bf16[4,96,768]{2,1,0:T(8,128)(2,1)S(1)} %get-tuple-element.35) | copy-start | bytes 1769476
  209.3 15.4 %copy-start.7 = (bf16[2,96,768]{2,1,0:T(8,128)(2,1)}, bf16[2,96,768]{2,1,0:T(8,128)(2,1)S(1)}, u32[]{:S(2)}) copy-start(bf16[2,96,768]{2,1,0:T(8,128)(2,1)S(1)} %get-tuple-element.37) | copy-start | bytes 884740
  209.3 18.3 %collective-permute-start.12 = (bf16[4,96,768]{2,1,0:T(8,128)(2,1)S(1)}, bf16[4,96,768]{2,1,0:T(8,128)(2,1)S(1)}, u32[]{:S(2)}, u32[]{:S(2)}) collective-permute-start(bf16[4,96,768]{2,1,0:T(8,128)(2,1)S(1)} %get-tuple-element.36), channel_id=1, source_target_pairs={{0,48},{16,0},{32,16},{48,32},{64,112},{80,64},{96,80},{112,96},{1... | collective-permute-start | bytes 1769480 | tf_op jit(solution)/shard_map/ppermute | solution.py:386
  224.6 0.8 copy-start.3
  225.5 26.4 %copy-start.4 = (bf16[4,48,1536]{2,1,0:T(8,128)(2,1)S(1)}, bf16[4,48,1536]{2,1,0:T(8,128)(2,1)}, u32[]{:S(2)}) copy-start(bf16[4,48,1536]{2,1,0:T(8,128)(2,1)} %copy-done.3) | copy-start | bytes 1769476
  225.5 13.0 %collective-permute-start = (bf16[4,48,1536]{2,1,0:T(8,128)(2,1)S(1)}, bf16[4,48,1536]{2,1,0:T(8,128)(2,1)S(1)}, u32[]{:S(2)}, u32[]{:S(2)}) collective-permute-start(bf16[4,48,1536]{2,1,0:T(8,128)(2,1)S(1)} %get-tuple-element.30), channel_id=1, source_target_pairs={{0,48},{16,0},{32,16},{48,32},{64,112},{80,64},{96,80},{112,96},{1... | collective-permute-start | bytes 1769480 | tf_op jit(solution)/shard_map/ppermute | solution.py:386
  226.3 16.8 %collective-permute-start.13 = (bf16[4,96,768]{2,1,0:T(8,128)(2,1)}, bf16[4,96,768]{2,1,0:T(8,128)(2,1)}, u32[]{:S(2)}, u32[]{:S(2)}) collective-permute-start(bf16[4,96,768]{2,1,0:T(8,128)(2,1)} %get-tuple-element.38), channel_id=1, source_target_pairs={{0,16},{16,32},{32,48},{48,0},{64,80},{80,96},{96,112},{112,64},{1... | collective-permute-start | bytes 1769480 | tf_op jit(solution)/shard_map/ppermute | solution.py:386
  227.5 24.3 %collective-permute-start.1 = (bf16[4,48,1536]{2,1,0:T(8,128)(2,1)}, bf16[4,48,1536]{2,1,0:T(8,128)(2,1)S(1)}, u32[]{:S(2)}, u32[]{:S(2)}) collective-permute-start(bf16[4,48,1536]{2,1,0:T(8,128)(2,1)} %get-tuple-element.32), channel_id=1, source_target_pairs={{0,16},{16,32},{32,48},{48,0},{64,80},{80,96},{96,112},{112,64},{1... | collective-permute-start | bytes 1769480 | tf_op jit(solution)/shard_map/ppermute | solution.py:386
  227.5 11.8 %copy-start.12 = (bf16[4,96,768]{2,1,0:T(8,128)(2,1)}, bf16[4,96,768]{2,1,0:T(8,128)(2,1)S(1)}, u32[]{:S(2)}) copy-start(bf16[4,96,768]{2,1,0:T(8,128)(2,1)S(1)} %collective-permute-done.12) | copy-start | bytes 1769476
  228.4 14.7 %collective-permute-start.15 = (bf16[2,96,768]{2,1,0:T(8,128)(2,1)}, bf16[2,96,768]{2,1,0:T(8,128)(2,1)}, u32[]{:S(2)}, u32[]{:S(2)}) collective-permute-start(bf16[2,96,768]{2,1,0:T(8,128)(2,1)} %add_convert_fusion.1), channel_id=1, source_target_pairs={{0,48},{16,0},{32,16},{48,32},{64,112},{80,64},{96,80},{112,96},{1... | collective-permute-start | bytes 884744 | tf_op jit(solution)/shard_map/ppermute | solution.py:386
  238.5 21.2 %copy-start.6 = (bf16[4,96,768]{2,1,0:T(8,128)(2,1)S(1)}, bf16[4,96,768]{2,1,0:T(8,128)(2,1)}, u32[]{:S(2)}) copy-start(bf16[4,96,768]{2,1,0:T(8,128)(2,1)} %copy-done.5) | copy-start | bytes 1769476
  239.3 12.5 %collective-permute-start.3 = (bf16[2,48,1536]{2,1,0:T(8,128)(2,1)}, bf16[2,48,1536]{2,1,0:T(8,128)(2,1)}, u32[]{:S(2)}, u32[]{:S(2)}) collective-permute-start(bf16[2,48,1536]{2,1,0:T(8,128)(2,1)} %add_convert_fusion.4), channel_id=1, source_target_pairs={{0,48},{16,0},{32,16},{48,32},{64,112},{80,64},{96,80},{112,96},{1... | collective-permute-start | bytes 884744 | tf_op jit(solution)/shard_map/ppermute | solution.py:386
  242.9 16.9 %copy-start.13 = (bf16[4,96,768]{2,1,0:T(8,128)(2,1)S(1)}, bf16[4,96,768]{2,1,0:T(8,128)(2,1)}, u32[]{:S(2)}) copy-start(bf16[4,96,768]{2,1,0:T(8,128)(2,1)} %copy-done.12) | copy-start | bytes 1769476
  244.6 15.1 %collective-permute-start.14 = (bf16[2,96,768]{2,1,0:T(8,128)(2,1)S(1)}, bf16[2,96,768]{2,1,0:T(8,128)(2,1)S(1)}, u32[]{:S(2)}, u32[]{:S(2)}) collective-permute-start(bf16[2,96,768]{2,1,0:T(8,128)(2,1)S(1)} %get-tuple-element.44), channel_id=1, source_target_pairs={{0,16},{16,32},{32,48},{48,0},{64,80},{80,96},{96,112},{112,64},{1... | collective-permute-start | bytes 884744 | tf_op jit(solution)/shard_map/ppermute | solution.py:386
  245.0 14.7 %collective-permute-start.16 = (bf16[2,96,768]{2,1,0:T(8,128)(2,1)S(1)}, bf16[2,96,768]{2,1,0:T(8,128)(2,1)S(1)}, u32[]{:S(2)}, u32[]{:S(2)}) collective-permute-start(bf16[2,96,768]{2,1,0:T(8,128)(2,1)S(1)} %get-tuple-element.45), channel_id=1, source_target_pairs={{0,64},{16,80},{32,96},{48,112},{64,0},{80,16},{96,32},{112,48},{1... | collective-permute-start | bytes 884744 | tf_op jit(solution)/shard_map/ppermute | solution.py:390
  253.0 17.9 %copy-start.15 = (f32[1,96,768]{2,1,0:T(8,128)S(1)}, f32[1,96,768]{2,1,0:T(8,128)}, u32[]{:S(2)}) copy-start(f32[1,96,768]{2,1,0:T(8,128)} %param.11) | copy-start | bytes 884740
  253.0 12.4 %collective-permute-start.2 = (bf16[2,48,1536]{2,1,0:T(8,128)(2,1)S(1)}, bf16[2,48,1536]{2,1,0:T(8,128)(2,1)S(1)}, u32[]{:S(2)}, u32[]{:S(2)}) collective-permute-start(bf16[2,48,1536]{2,1,0:T(8,128)(2,1)S(1)} %get-tuple-element.46), channel_id=1, source_target_pairs={{0,16},{16,32},{32,48},{48,0},{64,80},{80,96},{96,112},{112,64},{1... | collective-permute-start | bytes 884744 | tf_op jit(solution)/shard_map/ppermute | solution.py:386
  253.7 27.2 %copy-start.16 = (f32[1,48,1536]{2,1,0:T(8,128)S(1)}, f32[1,48,1536]{2,1,0:T(8,128)}, u32[]{:S(2)}) copy-start(f32[1,48,1536]{2,1,0:T(8,128)} %param.10) | copy-start | bytes 884740
  253.7 12.3 %collective-permute-start.4 = (bf16[2,48,1536]{2,1,0:T(8,128)(2,1)S(1)}, bf16[2,48,1536]{2,1,0:T(8,128)(2,1)S(1)}, u32[]{:S(2)}, u32[]{:S(2)}) collective-permute-start(bf16[2,48,1536]{2,1,0:T(8,128)(2,1)S(1)} %get-tuple-element.47), channel_id=1, source_target_pairs={{0,64},{16,80},{32,96},{48,112},{64,0},{80,16},{96,32},{112,48},{1... | collective-permute-start | bytes 884744 | tf_op jit(solution)/shard_map/ppermute | solution.py:390
  259.9 10.9 %collective-permute-start.17 = (bf16[96,768]{1,0:T(8,128)(2,1)S(1)}, bf16[96,768]{1,0:T(8,128)(2,1)S(1)}, u32[]{:S(2)}, u32[]{:S(2)}) collective-permute-start(bf16[96,768]{1,0:T(8,128)(2,1)S(1)} %fusion.9), channel_id=1, source_target_pairs={{0,128},{16,144},{32,160},{48,176},{64,192},{80,208},{96,224},{112... | collective-permute-start | bytes 442376 | tf_op jit(solution)/shard_map/ppermute | solution.py:390
  266.2 14.7 %collective-permute-start.5 = (bf16[48,1536]{1,0:T(8,128)(2,1)S(1)}, bf16[48,1536]{1,0:T(8,128)(2,1)S(1)}, u32[]{:S(2)}, u32[]{:S(2)}) collective-permute-start(bf16[48,1536]{1,0:T(8,128)(2,1)S(1)} %fusion.8), channel_id=1, source_target_pairs={{0,128},{16,144},{32,160},{48,176},{64,192},{80,208},{96,224},{112... | collective-permute-start | bytes 442376 | tf_op jit(solution)/shard_map/ppermute | solution.py:390
  272.6 10.8 %collective-permute-start.18 = (bf16[96,768]{1,0:T(8,128)(2,1)S(1)}, bf16[96,768]{1,0:T(8,128)(2,1)S(1)}, u32[]{:S(2)}, u32[]{:S(2)}) collective-permute-start(bf16[96,768]{1,0:T(8,128)(2,1)S(1)} %get-tuple-element.41), channel_id=1, source_target_pairs={{0,128},{16,144},{32,160},{48,176},{64,192},{80,208},{96,224},{112... | collective-permute-start | bytes 442376 | tf_op jit(solution)/shard_map/ppermute | solution.py:390
  282.6 7.9 %collective-permute-start.6 = (bf16[48,1536]{1,0:T(8,128)(2,1)S(1)}, bf16[48,1536]{1,0:T(8,128)(2,1)S(1)}, u32[]{:S(2)}, u32[]{:S(2)}) collective-permute-start(bf16[48,1536]{1,0:T(8,128)(2,1)S(1)} %get-tuple-element.43), channel_id=1, source_target_pairs={{0,128},{16,144},{32,160},{48,176},{64,192},{80,208},{96,224},{112... | collective-permute-start | bytes 442376 | tf_op jit(solution)/shard_map/ppermute | solution.py:390
  283.4 12.4 %collective-permute-start.19 = (bf16[2,96,768]{2,1,0:T(8,128)(2,1)S(1)}, bf16[2,96,768]{2,1,0:T(8,128)(2,1)S(1)}, u32[]{:S(2)}, u32[]{:S(2)}) collective-permute-start(bf16[2,96,768]{2,1,0:T(8,128)(2,1)S(1)} %pad_maximum_fusion.3), channel_id=1, source_target_pairs={{0,64},{16,80},{32,96},{48,112},{64,0},{80,16},{96,32},{112,48},{1... | collective-permute-start | bytes 884744 | tf_op jit(solution)/shard_map/ppermute | solution.py:390
  290.5 10.7 %collective-permute-start.7 = (bf16[2,48,1536]{2,1,0:T(8,128)(2,1)S(1)}, bf16[2,48,1536]{2,1,0:T(8,128)(2,1)S(1)}, u32[]{:S(2)}, u32[]{:S(2)}) collective-permute-start(bf16[2,48,1536]{2,1,0:T(8,128)(2,1)S(1)} %pad_maximum_fusion.2), channel_id=1, source_target_pairs={{0,64},{16,80},{32,96},{48,112},{64,0},{80,16},{96,32},{112,48},{1... | collective-permute-start | bytes 884744 | tf_op jit(solution)/shard_map/ppermute | solution.py:390
  295.9 17.6 %collective-permute-start.21 = (bf16[4,96,768]{2,1,0:T(8,128)(2,1)S(1)}, bf16[4,96,768]{2,1,0:T(8,128)(2,1)S(1)}, u32[]{:S(2)}, u32[]{:S(2)}) collective-permute-start(bf16[4,96,768]{2,1,0:T(8,128)(2,1)S(1)} %pad_maximum_fusion.1.home), channel_id=1, source_target_pairs={{0,16},{16,32},{32,48},{48,0},{64,80},{80,96},{96,112},{112,64},{1... | collective-permute-start | bytes 1769480 | tf_op jit(solution)/shard_map/ppermute | solution.py:386
  296.0 17.6 %collective-permute-start.20 = (bf16[4,96,768]{2,1,0:T(8,128)(2,1)S(1)}, bf16[4,96,768]{2,1,0:T(8,128)(2,1)S(1)}, u32[]{:S(2)}, u32[]{:S(2)}) collective-permute-start(bf16[4,96,768]{2,1,0:T(8,128)(2,1)S(1)} %pad_maximum_fusion.1.home), channel_id=1, source_target_pairs={{0,48},{16,0},{32,16},{48,32},{64,112},{80,64},{96,80},{112,96},{1... | collective-permute-start | bytes 1769480 | tf_op jit(solution)/shard_map/ppermute | solution.py:386
  301.4 24.7 %collective-permute-start.9 = (bf16[4,48,1536]{2,1,0:T(8,128)(2,1)S(1)}, bf16[4,48,1536]{2,1,0:T(8,128)(2,1)S(1)}, u32[]{:S(2)}, u32[]{:S(2)}) collective-permute-start(bf16[4,48,1536]{2,1,0:T(8,128)(2,1)S(1)} %pad_maximum_fusion.home), channel_id=1, source_target_pairs={{0,16},{16,32},{32,48},{48,0},{64,80},{80,96},{96,112},{112,64},{1... | collective-permute-start | bytes 1769480 | tf_op jit(solution)/shard_map/ppermute | solution.py:386
  301.5 24.8 %collective-permute-start.8 = (bf16[4,48,1536]{2,1,0:T(8,128)(2,1)S(1)}, bf16[4,48,1536]{2,1,0:T(8,128)(2,1)S(1)}, u32[]{:S(2)}, u32[]{:S(2)}) collective-permute-start(bf16[4,48,1536]{2,1,0:T(8,128)(2,1)S(1)} %pad_maximum_fusion.home), channel_id=1, source_target_pairs={{0,48},{16,0},{32,16},{48,32},{64,112},{80,64},{96,80},{112,96},{1... | collective-permute-start | bytes 1769480 | tf_op jit(solution)/shard_map/ppermute | solution.py:386
  313.5 18.9 %collective-permute-start.22 = (bf16[2,96,768]{2,1,0:T(8,128)(2,1)S(1)}, bf16[2,96,768]{2,1,0:T(8,128)(2,1)S(1)}, u32[]{:S(2)}, u32[]{:S(2)}) collective-permute-start(bf16[2,96,768]{2,1,0:T(8,128)(2,1)S(1)} %slice.158), channel_id=1, source_target_pairs={{0,16},{16,32},{32,48},{48,0},{64,80},{80,96},{96,112},{112,64},{1... | collective-permute-start | bytes 884744 | tf_op jit(solution)/shard_map/ppermute | solution.py:386
  313.6 18.8 %collective-permute-start.23 = (bf16[2,96,768]{2,1,0:T(8,128)(2,1)S(1)}, bf16[2,96,768]{2,1,0:T(8,128)(2,1)S(1)}, u32[]{:S(2)}, u32[]{:S(2)}) collective-permute-start(bf16[2,96,768]{2,1,0:T(8,128)(2,1)S(1)} %slice.159), channel_id=1, source_target_pairs={{0,48},{16,0},{32,16},{48,32},{64,112},{80,64},{96,80},{112,96},{1... | collective-permute-start | bytes 884744 | tf_op jit(solution)/shard_map/ppermute | solution.py:386
  326.1 10.0 %collective-permute-start.10 = (bf16[2,48,1536]{2,1,0:T(8,128)(2,1)S(1)}, bf16[2,48,1536]{2,1,0:T(8,128)(2,1)S(1)}, u32[]{:S(2)}, u32[]{:S(2)}) collective-permute-start(bf16[2,48,1536]{2,1,0:T(8,128)(2,1)S(1)} %slice.148), channel_id=1, source_target_pairs={{0,16},{16,32},{32,48},{48,0},{64,80},{80,96},{96,112},{112,64},{1... | collective-permute-start | bytes 884744 | tf_op jit(solution)/shard_map/ppermute | solution.py:386
  326.3 9.8 %collective-permute-start.11 = (bf16[2,48,1536]{2,1,0:T(8,128)(2,1)S(1)}, bf16[2,48,1536]{2,1,0:T(8,128)(2,1)S(1)}, u32[]{:S(2)}, u32[]{:S(2)}) collective-permute-start(bf16[2,48,1536]{2,1,0:T(8,128)(2,1)S(1)} %slice.149), channel_id=1, source_target_pairs={{0,48},{16,0},{32,16},{48,32},{64,112},{80,64},{96,80},{112,96},{1... | collective-permute-start | bytes 884744 | tf_op jit(solution)/shard_map/ppermute | solution.py:386
